TPU v7x, 256 devices: a whole 4x4x8 slice. The times are simulated.
256 devices in a mesh: noise: 8 (over x, core), dp: 32 (over y, z).
Axes of the slice: x: 4, y: 4, z: 8, core: 2. Of those that a mesh axis runs over, the one named last changes fastest.
Arguments:
- noise_latents: bfloat16 [32768, 128], P('noise'), may hold values from -6 to 6
- data_latents: bfloat16 [65536, 128], P('dp'), may hold values from -6 to 6
- projection: bfloat16 [128, 64], replicated, may hold values from -0.5 to 0.5
Outputs:
- targets: float32 [32768, 128], P(('noise', 'dp'))
- data_side_potential: float32 [65536], P('dp')
All inputs are finite; a program needn't handle non-finite values.
Results may differ from a plain program's by a relative error of at most 0.015.
The roundings to bfloat16 on the way count: a program that leaves them out, or rounds other values in their place, can miss the bound.
Values sent between devices are 32-bit elements; how exact they have to be, the bound alone decides.
A program may use at most 192 MiB of HBM per device.

v0:
```python
import math

import jax
import jax.numpy as jnp
from jax import lax
from jax.sharding import PartitionSpec as P

epsilon = 0.02


def joined(part, axis, combine):
    gathered = jax.tree.map(lambda a: lax.all_gather(a, axis), part)

    def take(source):
        return jax.tree.map(lambda a: lax.dynamic_index_in_dim(a, source, 0, False), gathered)

    return lax.fori_loop(
        1, lax.axis_size(axis), lambda source, state: combine(state, take(source)), take(0)
    )


def project_latents(latent_codes, projection):
    return jnp.dot(latent_codes, projection, preferred_element_type=jnp.float32).astype(
        jnp.bfloat16
    )


def tile_costs(qrows, rcols, rnorm):
    qnorm = jnp.sum(qrows.astype(jnp.float32) ** 2, axis=1)
    cross = lax.dot_general(
        qrows, rcols, (((1,), (1,)), ((), ())), preferred_element_type=jnp.float32
    )
    return (qnorm[:, None] + rnorm[None, :] - 2.0 * cross) / qrows.shape[1]


def combine_pair(first, second):
    top = jnp.maximum(first[0], second[0])
    return (top, first[1] * jnp.exp(first[0] - top) + second[1] * jnp.exp(second[0] - top))


def shards(noise_latents, data_latents, projection):
    qrows = project_latents(noise_latents, projection)
    rcols = project_latents(data_latents, projection)
    rnorm = jnp.sum(rcols.astype(jnp.float32) ** 2, axis=1)
    rows = qrows.shape[0]
    cols = rcols.shape[0]
    block = math.gcd(rows, 512)
    nblocks = rows // block
    total_rows = rows * lax.axis_size("noise")
    total_cols = cols * lax.axis_size("dp")
    qblocks = qrows.reshape(nblocks, block, qrows.shape[1])

    def column_update(frow):
        fblocks = frow.reshape(nblocks, block)

        def step(carry, index):
            top, total = carry
            z_vals = (fblocks[index][:, None] - tile_costs(qblocks[index], rcols, rnorm)) / epsilon
            new_top = jnp.maximum(top, jnp.max(z_vals, axis=0))
            total = total * jnp.exp(top - new_top) + jnp.sum(
                jnp.exp(z_vals - new_top[None, :]), axis=0
            )
            return ((new_top, total), None)

        start = (jnp.full((cols,), -1e30, jnp.float32), jnp.zeros((cols,), jnp.float32))
        (top, total), unused = lax.scan(step, start, jnp.arange(nblocks))
        top, total = joined((top, total), "noise", combine_pair)
        return -epsilon * (top + jnp.log(total) - math.log(total_rows))

    def row_block(gcol, qblock):
        z_vals = (gcol[None, :] - tile_costs(qblock, rcols, rnorm)) / epsilon
        top = jnp.max(z_vals, axis=1)
        return (top, jnp.sum(jnp.exp(z_vals - top[:, None]), axis=1))

    initial_data_dual = column_update(jnp.zeros((rows,), jnp.float32))
    local_top, local_sum = lax.map(lambda qb: row_block(initial_data_dual, qb), qblocks)
    local_top = local_top.reshape(rows)
    local_sum = local_sum.reshape(rows)
    row_top = lax.pmax(local_top, "dp")
    row_total = lax.psum(local_sum * jnp.exp(local_top - row_top), "dp")
    f_first = -epsilon * (row_top + jnp.log(row_total) - math.log(total_cols))
    data_side_potential = column_update(f_first)

    def final_block(qblock):
        z_vals = (data_side_potential[None, :] - tile_costs(qblock, rcols, rnorm)) / epsilon
        top = jnp.max(z_vals, axis=1)
        weights = jnp.exp(z_vals - top[:, None])
        den = jnp.sum(weights, axis=1)
        num = jnp.dot(
            weights.astype(jnp.bfloat16), data_latents, preferred_element_type=jnp.float32
        )
        return (top, den, num)

    block_top, block_den, block_num = lax.map(final_block, qblocks)
    block_top = block_top.reshape(rows)
    block_den = block_den.reshape(rows)
    block_num = block_num.reshape(rows, data_latents.shape[1])
    row_best = lax.pmax(block_top, "dp")
    scale = jnp.exp(block_top - row_best)
    num_share, den_share = (
        lax.psum_scatter(block_num * scale[:, None], "dp", scatter_dimension=0, tiled=True),
        lax.psum_scatter(block_den * scale, "dp", scatter_dimension=0, tiled=True),
    )
    targets = num_share / den_share[:, None]
    return (targets, data_side_potential)


def solution(mesh):
    in_specs = (P("noise", None), P("dp", None), P())
    out_specs = (P(("noise", "dp"), None), P("dp"))
    return jax.shard_map(shards, mesh=mesh, in_specs=in_specs, out_specs=out_specs, check_vma=False)
```

profile of v0, /device:TPU:1, one launch (start us, length us, event | category | flops | bytes accessed | tf_op | source)
XLA Modules:
  0.0 888.2 jit_solution(5120424220191588187)
XLA Ops:
  10.7 69.0 %while.90 = (s32[]{:T(128)}, f32[2048]{0:T(1024)S(1)}, f32[2048]{0:T(1024)S(1)}, s32[8]{0:T(128)S(1)}, bf16[8,512,64]{2,1,0:T(8,128)(2,1)S(1)}, /*index=5*/f32[2...) while((s32[]{:T(128)}, f32[2048]{0:T(1024)S(1)}, ...), condition=%wide.region_5.6_spmd.clone, body=%wide.region_1.5_spmd.clone.sunk | while | flops 143762944 | bytes 9228454 | solution.py:66
  13.4 3.1 fusion.62
  16.5 2.8 exponential_reduce_fusion.7
  22.0 3.1 fusion.62
  25.1 2.8 exponential_reduce_fusion.7
  30.6 3.1 fusion.62
  39.2 3.1 fusion.62
  47.9 3.1 fusion.62
  56.5 3.1 fusion.62
  65.1 3.1 fusion.62
  73.8 3.1 fusion.62
  79.7 15.8 %all-gather = f32[16384]{0:T(1024)S(1)} all-gather(f32[2048]{0:T(1024)S(1)} %get-tuple-element.436), channel_id=2, replica_groups=mesh['noise'=8,'dp'=32] {'noise'}, dimensions={0}, use_global_device_ids=true | all-gather | bytes 73728 | tf_op jit(solution)/shard_map/all_gather | solution.py:12
  95.5 12.8 %all-gather.1 = f32[16384]{0:T(1024)S(1)} all-gather(f32[2048]{0:T(1024)S(1)} %get-tuple-element.437), channel_id=3, replica_groups=mesh['noise'=8,'dp'=32] {'noise'}, dimensions={0}, use_global_device_ids=true | all-gather | bytes 73728 | tf_op jit(solution)/shard_map/all_gather | solution.py:12
  108.8 18.2 %while.87 = (s32[]{:T(128)}, f32[8,512]{1,0:T(8,128)S(1)}, f32[8,512]{1,0:T(8,128)S(1)}, f32[2048]{0:T(1024)S(1)}, bf16[8,512,64]{2,1,0:T(8,128)(2,1)S(1)}, /*in...) while((s32[]{:T(128)}, f32[8,512]{1,0:T(8,128)S(1)}, f32[8,512]{1,0:T(8,128)S(1)}, ...), condition=%wide.region_12.13_spmd, body=%wide.region_8.12_spmd.sunk | while | flops 143751680 | bytes 9144429 | solution.py:76
  127.1 117.1 %pmax.14 = f32[4096]{0:T(1024)S(1)} all-reduce(f32[4096]{0:T(1024)S(1)} %bitcast.121), channel_id=1, replica_groups=mesh['noise'=8,'dp'=32] {'dp'}, use_global_device_ids=true, to_apply=%region_13.14 | all-reduce | flops 4096 | bytes 32768 | tf_op jit(solution)/shard_map/pmax | solution.py:79
  244.2 110.4 %psum.7 = f32[4096]{0:T(1024)S(1)} all-reduce(f32[4096]{0:T(1024)S(1)} %exponential_multiply_fusion), channel_id=1, replica_groups=mesh['noise'=8,'dp'=32] {'dp'}, use_global_device_ids=true, to_apply=%region_14.15 | all-reduce | flops 4096 | bytes 32768 | tf_op jit(solution)/shard_map/psum | solution.py:80
  354.6 69.2 %while.91 = (s32[]{:T(128)}, f32[2048]{0:T(1024)S(1)}, f32[2048]{0:T(1024)S(1)}, s32[8]{0:T(128)S(1)}, f32[8,512]{1,0:T(8,128)S(1)}, /*index=5*/bf16[8,512,64]{2...) while((s32[]{:T(128)}, f32[2048]{0:T(1024)S(1)}, ...), condition=%wide.region_19.20_spmd.clone, body=%wide.region_15.19_spmd.clone.sunk | while | flops 143762944 | bytes 9234610 | solution.py:66
  357.3 3.1 fusion.65
  366.0 3.1 fusion.65
  374.6 3.1 fusion.65
  383.3 3.1 fusion.65
  391.9 3.1 fusion.65
  400.6 3.1 fusion.65
  409.2 3.1 fusion.65
  417.9 3.1 fusion.65
  423.8 67.5 %all-gather.2 = f32[16384]{0:T(1024)S(1)} all-gather(f32[2048]{0:T(1024)S(1)} %get-tuple-element.442), channel_id=4, replica_groups=mesh['noise'=8,'dp'=32] {'noise'}, dimensions={0}, use_global_device_ids=true | all-gather | bytes 73728 | tf_op jit(solution)/shard_map/all_gather | solution.py:12
  491.3 12.9 %all-gather.3 = f32[16384]{0:T(1024)S(1)} all-gather(f32[2048]{0:T(1024)S(1)} %get-tuple-element.443), channel_id=5, replica_groups=mesh['noise'=8,'dp'=32] {'noise'}, dimensions={0}, use_global_device_ids=true | all-gather | bytes 73728 | tf_op jit(solution)/shard_map/all_gather | solution.py:12
  504.8 30.1 %while.89 = (s32[]{:T(128)}, f32[8,512]{1,0:T(8,128)S(1)}, f32[8,512]{1,0:T(8,128)S(1)}, f32[8,512,128]{2,1,0:T(8,128)}, f32[2048]{0:T(1024)S(1)}, /*index=5*/bf...) while((s32[]{:T(128)}, f32[8,512]{1,0:T(8,128)S(1)}, ...), condition=%wide.region_26.27_spmd, body=%wide.region_22.26_spmd.sunk | while | flops 414284288 | bytes 14127741 | solution.py:94
  535.0 110.3 %pmax.15 = f32[4096]{0:T(1024)S(1)} all-reduce(f32[4096]{0:T(1024)S(1)} %bitcast.119), channel_id=1, replica_groups=mesh['noise'=8,'dp'=32] {'dp'}, use_global_device_ids=true, to_apply=%region_27.28 | all-reduce | flops 4096 | bytes 32768 | tf_op jit(solution)/shard_map/pmax | solution.py:98
  645.3 3.5 bitcast_multiply_fusion
  650.1 110.4 %all-reduce = f32[4096]{0:T(1024)S(1)} all-reduce(f32[4096]{0:T(1024)S(1)} %get-tuple-element.648), channel_id=7, replica_groups=mesh['noise'=8,'dp'=32] {'dp'}, use_global_device_ids=true, to_apply=%region_29.30.clone | all-reduce | flops 4096 | bytes 32768
  760.5 119.3 %reduce-scatter.2.cloned.1.call-done = f32[128,128]{1,0:T(8,128)} async-done(((f32[4096,128]{1,0:T(8,128)}), f32[128,128]{1,0:T(8,128)}) %reduce-scatter.2.cloned.1.call-update) | async-done | bytes 65552 | tf_op jit(solution)/shard_map/reduce_scatter | solution.py:101
  (266 shorter events, 106.1 us)
Async XLA Ops:
  7.2 1.8 copy-start
  7.2 872.6 %reduce-scatter.2.cloned.1.call-start = ((), (), s32[]{:S(2)}) async-start(), calls=%async_computation.1 | async-start | bytes 2162688 | tf_op jit(solution)/shard_map/reduce_scatter | solution.py:101
  354.6 150.2 %copy-start.1 = (bf16[2048,128]{1,0:T(8,128)(2,1)S(1)}, bf16[2048,128]{1,0:T(8,128)(2,1)}, u32[]{:S(2)}) copy-start(bf16[2048,128]{1,0:T(8,128)(2,1)} %param.16) | copy-start | bytes 1572868
  534.9 346.4 %copy-start.2 = (f32[2048]{0:T(1024)}, f32[2048]{0:T(1024)S(1)}, u32[]{:S(2)}) copy-start(f32[2048]{0:T(1024)S(1)} %get-tuple-element.1132) | copy-start | bytes 24580
  534.9 113.9 %copy-start.3 = (u32[256]{0:T(256)S(1)}, u32[256]{0:T(256)}, u32[]{:S(2)}) copy-start(u32[256]{0:T(256)} %constant.192) | copy-start | bytes 3076
Sparse Core Ops, SparseCore 0:
  649.0 230.7 reduce-scatter.1
where the time goes:
time: 894 us; the launch traced here: 888 us
  blocking collectives  557 us (62%)
  waiting for transfers between devices  119 us (13%)
  matrix products  84.6 us (9%)
  other arithmetic  66.2 us (7%)
  loops' own time  32.7 us (4%)
  between operations  15 us (2%)
  local copies, waits for them, and re-layouts  13.2 us (1%)
    reduce_scatter x1, waiting for transfers between devices, shards(): lax.psum_scatter(block_num * scale[:, None], 'dp', scatter_dimension=0, t...  119 us
    pmax x1, blocking collectives, shards(): row_top = lax.pmax(local_top, 'dp')  117 us
    psum x1, blocking collectives, shards(): row_total = lax.psum(local_sum * jnp.exp(local_top - row_top), 'dp')  110 us
    unnamed x1, blocking collectives  110 us
    pmax x1, blocking collectives, shards(): row_best = lax.pmax(block_top, 'dp')  110 us
    all_gather x4, blocking collectives, joined(): gathered = jax.tree.map(lambda a: lax.all_gather(a, axis), part)  109 us
    dot_general x32, matrix products, tile_costs(): lax.dot_general(qrows, rcols, (((1,), (1,)), ((), ())), preferred_element...  70 us
    reduce_sum x16, other arithmetic, step(): jnp.sum(jnp.exp(z_vals - new_top[None, :]), axis=0)  44.5 us
  transfers between devices with their start and end apart: 1, of which 1 were waited for; matrix products, arithmetic and copies ran while one was open for 0% of the time, Pallas kernels for 0%

commit v1 on v0

v1 whole, which is shorter than its diff:
```python
import functools
import math

import jax
import jax.numpy as jnp
from jax import lax
from jax.experimental import pallas as pl
from jax.experimental.pallas import tpu as pltpu
from jax.sharding import PartitionSpec as P

epsilon = 0.02
LOG2E = 1.0 / math.log(2.0)
LN2 = math.log(2.0)
NT = (((1,), (1,)), ((), ()))
MESH = pl.DeviceIdType.MESH
LANES = 128


def ring_sizes(dp):
    return {32: (4, 8), 8: (2, 4), 16: (4, 4)}[dp]


def split3(x):
    hi = x.astype(jnp.bfloat16).astype(jnp.float32)
    rest = x - hi
    mid = rest.astype(jnp.bfloat16).astype(jnp.float32)
    return hi, mid, rest - mid


def kernel(
    cfg,
    noise_ref,
    data_ref,
    proj_ref,
    targets_ref,
    pot_ref,
    q_ref,
    r_ref,
    p_ref,
    d_ref,
    proj2_ref,
    ul_ref,
    vl_ref,
    st1_ref,
    st2_ref,
    rb2_ref,
    f_ref,
    st3_ref,
    num1_ref,
    num2_ref,
    ry1_ref,
    rz1_ref,
    rz2_ref,
    ry2_ref,
    s1_send,
    s1_recv,
    s2_send,
    s2_recv,
    sf_send,
    sf_recv,
    s3_send,
    s3_recv,
    y1_sem,
    z1_sem,
    z2_sem,
    y2_sem,
):
    rows, cols, n_noise, n_dp, kdim = cfg
    ys, zs = ring_sizes(n_dp)
    rch, cch = rows // LANES, cols // LANES
    log_rows = math.log2(rows * n_noise)
    log_cols = math.log2(cols * n_dp)
    scale = 2.0 * LOG2E / (kdim * epsilon)
    norm_scale = LOG2E / (kdim * epsilon)
    me_n = lax.axis_index("noise")
    me_d = lax.axis_index("dp")
    me_y, me_z = me_d // zs, me_d % zs

    barrier = pltpu.get_barrier_semaphore()

    def greet_noise(k, carry):
        pl.semaphore_signal(
            barrier, inc=1, device_id=((me_n + k) % n_noise, me_d), device_id_type=MESH
        )
        return carry

    def greet_dp(k, carry):
        pl.semaphore_signal(
            barrier, inc=1, device_id=(me_n, (me_d + k) % n_dp), device_id_type=MESH
        )
        return carry

    lax.fori_loop(1, n_noise, greet_noise, 0)
    lax.fori_loop(1, n_dp, greet_dp, 0)

    proj2_ref[:, 0:kdim] = proj_ref[...]
    proj2_ref[:, kdim : 2 * kdim] = proj_ref[...]
    half = jnp.full((8, LANES), 0.5, jnp.bfloat16)
    one = jnp.ones((1, LANES), jnp.float32)
    zero = jnp.zeros((2, LANES), jnp.float32)

    def put_bias(dst_ref, c, bias, first):
        parts = list(split3(bias))
        ones = [one, one, one]
        tile = jnp.concatenate((parts + ones if first else ones + parts) + [zero], axis=0)
        dst_ref[c * LANES : (c + 1) * LANES, 128:136] = tile.T.astype(jnp.bfloat16)

    def prepare(src_ref, dst_ref, bias_ref, count, is_q):
        step = min(512, count)

        def body(b, carry):
            sl = pl.ds(pl.multiple_of(b * step, step), step)
            proj = jnp.dot(src_ref[sl, :], proj2_ref[...], preferred_element_type=jnp.float32)
            code = proj.astype(jnp.bfloat16)
            full = code.astype(jnp.float32)
            square = full * full
            sq_hi = square.astype(jnp.bfloat16)
            sq_lo = (square - sq_hi.astype(jnp.float32)).astype(jnp.bfloat16)
            norm = lax.dot_general(
                half, sq_hi, NT, preferred_element_type=jnp.float32
            ) + lax.dot_general(half, sq_lo, NT, preferred_element_type=jnp.float32)
            if is_q:
                dst_ref[sl, 0:128] = code
            else:
                scaled = full * scale
                hi = scaled.astype(jnp.bfloat16)
                lo = (scaled - hi.astype(jnp.float32)).astype(jnp.bfloat16)
                lane = lax.broadcasted_iota(jnp.int32, scaled.shape, 1)
                dst_ref[sl, 0:128] = jnp.where(
                    lane < kdim, hi.astype(jnp.float32), lo.astype(jnp.float32)
                ).astype(jnp.bfloat16)
            dst_ref[sl, 128:256] = jnp.zeros((step, 128), jnp.bfloat16)
            for c in range(step // LANES):
                bias_ref[pl.ds(b * (step // LANES) + c, 1), :] = (
                    -norm_scale * norm[0:1, c * LANES : (c + 1) * LANES]
                )
            return carry

        lax.fori_loop(0, count // step, body, 0)
        bias = bias_ref[...]
        for c in range(count // LANES):
            put_bias(dst_ref, c, bias[c : c + 1, :], is_q)

    prepare(noise_ref, q_ref, ul_ref, rows, True)
    prepare(data_ref, r_ref, vl_ref, cols, False)

    def lse_pass(lhs_ref, count, rhs_ref, width, write):
        bw = min(2048, width)
        bl = 256
        un = 2

        def wide(w, carry):
            rhs = rhs_ref[pl.ds(pl.multiple_of(w * bw, bw), bw), :]

            def body(step, state):
                top, total = state
                for u in range(un):
                    sl = pl.ds(pl.multiple_of((step * un + u) * bl, bl), bl)
                    z = lax.dot_general(
                        lhs_ref[sl, :], rhs, NT, preferred_element_type=jnp.float32
                    ).reshape(bl // 8, 8, bw)
                    new = jnp.maximum(top, jnp.max(z, axis=0))
                    total = total * jnp.exp2(top - new) + jnp.sum(jnp.exp2(z - new[None]), axis=0)
                    top = new
                return top, total

            start = (jnp.full((8, bw), -1e30, jnp.float32), jnp.zeros((8, bw), jnp.float32))
            top, total = lax.fori_loop(0, count // (bl * un), body, start)
            best = jnp.max(top, axis=0, keepdims=True)
            write(w, bw, best, jnp.sum(total * jnp.exp2(top - best), axis=0, keepdims=True))
            return carry

        lax.fori_loop(0, width // bw, wide, 0)

    def write1(w, bw, top, total):
        for c in range(bw // LANES):
            lanes = slice(c * LANES, (c + 1) * LANES)
            st1_ref[me_n, 0, pl.ds(w * (bw // LANES) + c, 1), :] = top[:, lanes]
            st1_ref[me_n, 1, pl.ds(w * (bw // LANES) + c, 1), :] = total[:, lanes]

    def write2(w, bw, top, total):
        for c in range(bw // LANES):
            lanes = slice(c * LANES, (c + 1) * LANES)
            st2_ref[w * (bw // LANES) + c, 0:1, :] = top[:, lanes]
            st2_ref[w * (bw // LANES) + c, 1:2, :] = total[:, lanes]

    lse_pass(q_ref, rows, r_ref, cols, write1)
    pl.semaphore_wait(barrier, n_noise - 1 + n_dp - 1)

    def gather_noise(ref, send_sem, recv_sem):
        def copy(k):
            return pltpu.make_async_remote_copy(
                src_ref=ref.at[me_n],
                dst_ref=ref.at[me_n],
                send_sem=send_sem.at[k],
                recv_sem=recv_sem.at[me_n],
                device_id=((me_n + k) % n_noise, me_d),
                device_id_type=MESH,
            )

        def start(k, carry):
            copy(k).start()
            return carry

        def wait(k, carry):
            source = (me_n + n_noise - k) % n_noise
            pltpu.make_async_copy(ref.at[source], ref.at[source], recv_sem.at[source]).wait()
            copy(k).wait_send()
            return carry

        lax.fori_loop(1, n_noise, start, 0)
        lax.fori_loop(1, n_noise, wait, 0)

    gather_noise(st1_ref, s1_send, s1_recv)
    top = st1_ref[0, 0]
    for k in range(1, n_noise):
        top = jnp.maximum(top, st1_ref[k, 0])
    total = st1_ref[0, 1] * jnp.exp2(st1_ref[0, 0] - top)
    for k in range(1, n_noise):
        total = total + st1_ref[k, 1] * jnp.exp2(st1_ref[k, 0] - top)
    g1 = log_rows - (top + jnp.log(total) * LOG2E)
    vl = vl_ref[...] + g1
    for c in range(cch):
        put_bias(r_ref, c, vl[c : c + 1, :], False)

    lse_pass(r_ref, cols, q_ref, rows, write2)

    def scatter(k):
        other = (me_d + k) % n_dp
        return pltpu.make_async_remote_copy(
            src_ref=st2_ref.at[other],
            dst_ref=rb2_ref.at[me_d],
            send_sem=s2_send.at[k],
            recv_sem=s2_recv.at[me_d],
            device_id=(me_n, other),
            device_id_type=MESH,
        )

    def back(k):
        return pltpu.make_async_remote_copy(
            src_ref=f_ref.at[me_d],
            dst_ref=f_ref.at[me_d],
            send_sem=sf_send.at[k],
            recv_sem=sf_recv.at[me_d],
            device_id=(me_n, (me_d + k) % n_dp),
            device_id_type=MESH,
        )

    def start_scatter(k, carry):
        scatter(k).start()
        return carry

    def wait_scatter(k, carry):
        source = (me_d + n_dp - k) % n_dp
        pltpu.make_async_copy(rb2_ref.at[source], rb2_ref.at[source], s2_recv.at[source]).wait()
        scatter(k).wait_send()
        return carry

    def start_back(k, carry):
        back(k).start()
        return carry

    def wait_back(k, carry):
        source = (me_d + n_dp - k) % n_dp
        pltpu.make_async_copy(f_ref.at[source], f_ref.at[source], sf_recv.at[source]).wait()
        back(k).wait_send()
        return carry

    lax.fori_loop(1, n_dp, start_scatter, 0)
    rb2_ref[me_d] = st2_ref[me_d]
    lax.fori_loop(1, n_dp, wait_scatter, 0)
    tops = rb2_ref[:, 0, :]
    sums = rb2_ref[:, 1, :]
    top = jnp.max(tops, axis=0, keepdims=True)
    total = jnp.sum(sums * jnp.exp2(tops - top), axis=0, keepdims=True)
    f_ref[me_d] = log_cols - (top + jnp.log(total) * LOG2E)
    lax.fori_loop(1, n_dp, start_back, 0)
    lax.fori_loop(1, n_dp, wait_back, 0)
    ul = ul_ref[...]
    for c in range(rch):
        put_bias(q_ref, c, ul[c : c + 1, :] + f_ref[c], True)

    bl, bw, un = 256, cols, 2

    def plan(step, total):
        for u in range(un):
            sl = pl.ds(pl.multiple_of((step * un + u) * bl, bl), bl)
            z = lax.dot_general(q_ref[sl, :], r_ref[...], NT, preferred_element_type=jnp.float32)
            p = jnp.exp2(z)
            p_ref[sl, :] = p.astype(jnp.bfloat16)
            total = total + jnp.sum(p.reshape(bl // 8, 8, bw), axis=0)
        return total

    total = lax.fori_loop(0, rows // (bl * un), plan, jnp.zeros((8, bw), jnp.float32))
    total = jnp.sum(total, axis=0, keepdims=True)
    for c in range(cch):
        st3_ref[me_n, c : c + 1, :] = total[:, c * LANES : (c + 1) * LANES]
    gather_noise(st3_ref, s3_send, s3_recv)
    total = st3_ref[0]
    for k in range(1, n_noise):
        total = total + st3_ref[k]
    pot_ref[...] = (epsilon * LN2) * (g1 + log_rows - jnp.log(total) * LOG2E)

    factor = float(rows * n_noise) / total
    f_hi = factor.astype(jnp.bfloat16).astype(jnp.float32)
    f_lo = factor - f_hi
    zero5 = jnp.zeros((5, LANES), jnp.float32)
    for c in range(cch):
        sl = slice(c * LANES, (c + 1) * LANES)
        tile = jnp.concatenate(
            [f_hi[c : c + 1], f_lo[c : c + 1], factor[c : c + 1], zero5], axis=0
        ).T
        d_ref[sl, 0:128] = (data_ref[sl, :].astype(jnp.float32) * tile[:, 2:3]).astype(
            jnp.bfloat16
        )
        d_ref[sl, 128:256] = jnp.zeros((LANES, 128), jnp.bfloat16)
        d_ref[sl, 128:136] = tile.astype(jnp.bfloat16)

    def weigh(y, carry):
        n = zs * LANES
        sl = pl.ds(pl.multiple_of(y * n, n), n)
        both = jnp.dot(p_ref[sl, :], d_ref[...], preferred_element_type=jnp.float32)
        for z in range(zs):
            part = both[z * LANES : (z + 1) * LANES]
            num1_ref[y, z, 0:64, :] = part[0:64, 0:128]
            num1_ref[y, z, 64:72, :] = part[:, 128:136].T
            num2_ref[z, y, :, :] = part[64:128, 0:128]
        return carry

    lax.fori_loop(0, ys, weigh, 0)

    def ring(block, recv_ref, sem, size, me, peer, cut):
        h = size // 2
        right, left = peer((me + 1) % size), peer((me + size - 1) % size)

        def copies(k):
            ahead, behind = (me + k) % size, (me + size - k) % size
            first = block(ahead, slice(0, cut)) if k == h else block(ahead, None)
            second = block(behind, slice(cut, None)) if k == h else block(behind, None)
            land = [recv_ref.at[2 * (k - 1)], recv_ref.at[2 * (k - 1) + 1]]
            if k == h:
                land = [land[0].at[0:cut], land[1].at[cut : recv_ref.shape[1]]]
            out = []
            for i, (src, dst, dev) in enumerate(((first, land[0], right), (second, land[1], left))):
                out.append(
                    pltpu.make_async_remote_copy(
                        src_ref=src,
                        dst_ref=dst,
                        send_sem=sem.at[0, k - 1, i],
                        recv_sem=sem.at[1, k - 1, i],
                        device_id=dev,
                        device_id_type=MESH,
                    )
                )
            return out

        def add(k):
            for i, target in enumerate(((me + k - 1) % size, (me + size - k + 1) % size)):
                sl = None
                if k == h:
                    sl = slice(0, cut) if i == 0 else slice(cut, recv_ref.shape[1])
                dst = block(target, sl)
                src = recv_ref.at[2 * (k - 1) + i]
                if sl is not None:
                    src = src.at[sl]
                dst[...] = dst[...] + src[...]

        return copies, add, h

    def peer_y(y):
        return (me_n, y * zs + me_z)

    def peer_z(z):
        return (me_n, me_y * zs + z)

    def cutter(ref, extent):
        def block(index, sl):
            if sl is None:
                return ref.at[index]
            return ref.at[index, sl.start : (extent if sl.stop is None else sl.stop)]

        return block

    def run(stages):
        most = max(h for _, _, h in stages)
        for k in range(most, 0, -1):
            live = [(copies(k), add) for copies, add, h in stages if k <= h]
            for pair, _ in live:
                for c in pair:
                    c.start()
            for pair, add in live:
                for c in pair:
                    c.wait()
                add(k)

    run(
        [
            ring(cutter(num1_ref, zs), ry1_ref, y1_sem, ys, me_y, peer_y, zs // 2),
            ring(cutter(num2_ref, ys), rz2_ref, z2_sem, zs, me_z, peer_z, ys // 2),
        ]
    )
    run(
        [
            ring(cutter(num1_ref.at[me_y], 72), rz1_ref, z1_sem, zs, me_z, peer_z, 40),
            ring(cutter(num2_ref.at[me_z], 64), ry2_ref, y2_sem, ys, me_y, peer_y, 32),
        ]
    )
    mine = num1_ref[me_y, me_z]
    den = (mine[64:72]).T
    den = den[:, 0:1] + den[:, 1:2]
    targets_ref[0:64, :] = mine[0:64] / den[0:64]
    targets_ref[64:128, :] = num2_ref[me_z, me_y] / den[64:128]


def shards(noise_latents, data_latents, projection):
    rows, width = noise_latents.shape
    cols = data_latents.shape[0]
    kdim = projection.shape[1]
    n_noise, n_dp = lax.axis_size("noise"), lax.axis_size("dp")
    ys, zs = ring_sizes(n_dp)
    rch, cch = rows // LANES, cols // LANES
    f32, bf16 = jnp.float32, jnp.bfloat16
    cfg = (rows, cols, n_noise, n_dp, kdim)
    dma = pltpu.SemaphoreType.DMA
    vmem = pl.BlockSpec(memory_space=pltpu.VMEM)
    targets, pot = pl.pallas_call(
        functools.partial(kernel, cfg),
        out_shape=(
            jax.ShapeDtypeStruct((LANES, width), f32),
            jax.ShapeDtypeStruct((cch, LANES), f32),
        ),
        in_specs=[vmem] * 3,
        out_specs=(vmem, vmem),
        scratch_shapes=[
            pltpu.VMEM((rows, 256), bf16),
            pltpu.VMEM((cols, 256), bf16),
            pltpu.VMEM((rows, cols), bf16),
            pltpu.VMEM((cols, 256), bf16),
            pltpu.VMEM((width, 2 * kdim), bf16),
            pltpu.VMEM((rch, LANES), f32),
            pltpu.VMEM((cch, LANES), f32),
            pltpu.VMEM((n_noise, 2, cch, LANES), f32),
            pltpu.VMEM((n_dp, 2, LANES), f32),
            pltpu.VMEM((n_dp, 2, LANES), f32),
            pltpu.VMEM((n_dp, 1, LANES), f32),
            pltpu.VMEM((n_noise, cch, LANES), f32),
            pltpu.VMEM((ys, zs, 72, LANES), f32),
            pltpu.VMEM((zs, ys, 64, LANES), f32),
            pltpu.VMEM((ys, zs, 72, LANES), f32),
            pltpu.VMEM((zs, 72, LANES), f32),
            pltpu.VMEM((zs, ys, 64, LANES), f32),
            pltpu.VMEM((ys, 64, LANES), f32),
            dma((n_noise,)),
            dma((n_noise,)),
            dma((n_dp,)),
            dma((n_dp,)),
            dma((n_dp,)),
            dma((n_dp,)),
            dma((n_noise,)),
            dma((n_noise,)),
            dma((2, ys // 2, 2)),
            dma((2, zs // 2, 2)),
            dma((2, zs // 2, 2)),
            dma((2, ys // 2, 2)),
        ],
        compiler_params=pltpu.CompilerParams(
            collective_id=0, has_side_effects=True, vmem_limit_bytes=56 * 2**20
        ),
        cost_estimate=pl.CostEstimate(
            flops=8 * rows * cols * 256, bytes_accessed=2**21, transcendentals=3 * rows * cols
        ),
    )(noise_latents, data_latents, projection)
    return (targets, pot.reshape(cols))


def solution(mesh):
    in_specs = (P("noise", None), P("dp", None), P())
    out_specs = (P(("noise", "dp"), None), P("dp"))
    return jax.shard_map(shards, mesh=mesh, in_specs=in_specs, out_specs=out_specs, check_vma=False)
```

time: 894 us -> 104 us (0.12)
  the two profiles are of different devices: /device:TPU:1 before, /device:TPU:4 now
where the time goes in v1:
time: 104 us
  Pallas kernels  100 us (96%)
  local copies, waits for them, and re-layouts  3.52 us (3%)
    pallas_call x1, Pallas kernels, shards(): pl.pallas_call(functools.partial(kernel, cfg), out_shape=(jax.ShapeDtypeS...  100 us
    unnamed x5, local copies, waits for them, and re-layouts  3.52 us

profile of v1, /device:TPU:4, one launch (start us, length us, event | category | flops | bytes accessed | tf_op | source)
XLA Modules:
  0.0 104.2 jit_solution(9644041797941706458)
XLA Ops:
  0.6 1.4 %copy.5.proj_ref = bf16[128,64]{1,0:T(8,128)(2,1)} copy(bf16[128,64]{0,1:T(8,128)(2,1)} %param.5) | data formatting | bytes 32768 | tf_op args[2]
  2.1 100.0 %shard_map.50 = (f32[128,128]{1,0:T(8,128)}, f32[16,128]{1,0:T(8,128)}) custom-call(bf16[4096,128]{1,0:T(8,128)(2,1)} %noise_ref.1, bf16[2048,128]{1,0:T(8,128)(2,1)} %data_ref.1, bf16[128,64]{1,0:T(8,128)(2,1)} %copy.5.proj_ref), custom_call_target="tpu_custom_call" | custom-call | flops 17179869184 | bytes 2097152 | tf_op jit(solution)/shard_map/pallas_call | solution.py:426
  102.1 0.0 copy-start
  102.1 1.5 %copy.8 = f32[128,128]{1,0:T(8,128)} copy(f32[128,128]{1,0:T(8,128)} %get-tuple-element.8) | data formatting | bytes 131072
  103.6 0.0 copy-done
  103.6 0.6 copy.9
Async XLA Ops:
  102.1 1.5 %copy-start = (f32[16,128]{1,0:T(8,128)S(1)}, f32[16,128]{1,0:T(8,128)}, u32[]{:S(2)}) copy-start(f32[16,128]{1,0:T(8,128)} %get-tuple-element.5) | copy-start | bytes 24580

commit v2 on v1

--- a/solution.py
+++ b/solution.py
@@ -93,8 +93,8 @@
     lax.fori_loop(1, n_noise, greet_noise, 0)
     lax.fori_loop(1, n_dp, greet_dp, 0)
 
-    proj2_ref[:, 0:kdim] = proj_ref[...]
-    proj2_ref[:, kdim : 2 * kdim] = proj_ref[...]
+    proj2_ref[0:kdim, :] = proj_ref[...]
+    proj2_ref[kdim : 2 * kdim, :] = proj_ref[...]
     half = jnp.full((8, LANES), 0.5, jnp.bfloat16)
     one = jnp.ones((1, LANES), jnp.float32)
     zero = jnp.zeros((2, LANES), jnp.float32)
@@ -110,7 +110,9 @@
 
         def body(b, carry):
             sl = pl.ds(pl.multiple_of(b * step, step), step)
-            proj = jnp.dot(src_ref[sl, :], proj2_ref[...], preferred_element_type=jnp.float32)
+            proj = lax.dot_general(
+                src_ref[sl, :], proj2_ref[...], NT, preferred_element_type=jnp.float32
+            )
             code = proj.astype(jnp.bfloat16)
             full = code.astype(jnp.float32)
             square = full * full
@@ -147,7 +149,7 @@
     def lse_pass(lhs_ref, count, rhs_ref, width, write):
         bw = min(2048, width)
         bl = 256
-        un = 2
+        un = min(4, count // bl)
 
         def wide(w, carry):
             rhs = rhs_ref[pl.ds(pl.multiple_of(w * bw, bw), bw), :]
@@ -280,14 +282,20 @@
     for c in range(rch):
         put_bias(q_ref, c, ul[c : c + 1, :] + f_ref[c], True)
 
-    bl, bw, un = 256, cols, 2
+    bl, bw, un = 256, cols, min(4, rows // 256)
+    per = bl // LANES
 
     def plan(step, total):
         for u in range(un):
-            sl = pl.ds(pl.multiple_of((step * un + u) * bl, bl), bl)
+            tile = step * un + u
+            sl = pl.ds(pl.multiple_of(tile * bl, bl), bl)
             z = lax.dot_general(q_ref[sl, :], r_ref[...], NT, preferred_element_type=jnp.float32)
             p = jnp.exp2(z)
-            p_ref[sl, :] = p.astype(jnp.bfloat16)
+            half_p = p.astype(jnp.bfloat16)
+            for i in range(per):
+                chunk = tile * per + i
+                put = pl.ds(pl.multiple_of(chunk // zs * LANES, LANES), LANES)
+                p_ref[chunk % zs, put, :] = half_p[i * LANES : (i + 1) * LANES]
             total = total + jnp.sum(p.reshape(bl // 8, 8, bw), axis=0)
         return total
 
@@ -316,100 +324,146 @@
         d_ref[sl, 128:256] = jnp.zeros((LANES, 128), jnp.bfloat16)
         d_ref[sl, 128:136] = tile.astype(jnp.bfloat16)
 
-    def weigh(y, carry):
-        n = zs * LANES
-        sl = pl.ds(pl.multiple_of(y * n, n), n)
-        both = jnp.dot(p_ref[sl, :], d_ref[...], preferred_element_type=jnp.float32)
-        for z in range(zs):
-            part = both[z * LANES : (z + 1) * LANES]
-            num1_ref[y, z, 0:64, :] = part[0:64, 0:128]
-            num1_ref[y, z, 64:72, :] = part[:, 128:136].T
-            num2_ref[z, y, :, :] = part[64:128, 0:128]
-        return carry
-
-    lax.fori_loop(0, ys, weigh, 0)
-
-    def ring(block, recv_ref, sem, size, me, peer, cut):
-        h = size // 2
-        right, left = peer((me + 1) % size), peer((me + size - 1) % size)
-
-        def copies(k):
-            ahead, behind = (me + k) % size, (me + size - k) % size
-            first = block(ahead, slice(0, cut)) if k == h else block(ahead, None)
-            second = block(behind, slice(cut, None)) if k == h else block(behind, None)
-            land = [recv_ref.at[2 * (k - 1)], recv_ref.at[2 * (k - 1) + 1]]
-            if k == h:
-                land = [land[0].at[0:cut], land[1].at[cut : recv_ref.shape[1]]]
-            out = []
-            for i, (src, dst, dev) in enumerate(((first, land[0], right), (second, land[1], left))):
-                out.append(
-                    pltpu.make_async_remote_copy(
-                        src_ref=src,
-                        dst_ref=dst,
-                        send_sem=sem.at[0, k - 1, i],
-                        recv_sem=sem.at[1, k - 1, i],
-                        device_id=dev,
-                        device_id_type=MESH,
-                    )
-                )
-            return out
-
-        def add(k):
-            for i, target in enumerate(((me + k - 1) % size, (me + size - k + 1) % size)):
-                sl = None
-                if k == h:
-                    sl = slice(0, cut) if i == 0 else slice(cut, recv_ref.shape[1])
-                dst = block(target, sl)
-                src = recv_ref.at[2 * (k - 1) + i]
-                if sl is not None:
-                    src = src.at[sl]
-                dst[...] = dst[...] + src[...]
-
-        return copies, add, h
-
-    def peer_y(y):
-        return (me_n, y * zs + me_z)
-
-    def peer_z(z):
-        return (me_n, me_y * zs + z)
-
-    def cutter(ref, extent):
-        def block(index, sl):
-            if sl is None:
-                return ref.at[index]
-            return ref.at[index, sl.start : (extent if sl.stop is None else sl.stop)]
-
-        return block
-
-    def run(stages):
-        most = max(h for _, _, h in stages)
-        for k in range(most, 0, -1):
-            live = [(copies(k), add) for copies, add, h in stages if k <= h]
-            for pair, _ in live:
-                for c in pair:
-                    c.start()
-            for pair, add in live:
-                for c in pair:
-                    c.wait()
-                add(k)
-
-    run(
-        [
-            ring(cutter(num1_ref, zs), ry1_ref, y1_sem, ys, me_y, peer_y, zs // 2),
-            ring(cutter(num2_ref, ys), rz2_ref, z2_sem, zs, me_z, peer_z, ys // 2),
-        ]
-    )
-    run(
-        [
-            ring(cutter(num1_ref.at[me_y], 72), rz1_ref, z1_sem, zs, me_z, peer_z, 40),
-            ring(cutter(num2_ref.at[me_z], 64), ry2_ref, y2_sem, ys, me_y, peer_y, 32),
-        ]
-    )
-    mine = num1_ref[me_y, me_z]
+    h = zs // 2
+    offsets = [h]
+    for k in range(h - 1, 0, -1):
+        offsets += [k, zs - k]
+    offsets.append(0)
+    y_steps = [2, 1, 3] if ys == 4 else [1]
+    pending = []
+
+    def peer_y(step):
+        return (me_n, (me_y + step) % ys * zs + me_z)
+
+    def peer_z(step):
+        return (me_n, me_y * zs + (me_z + step) % zs)
+
+    def send(src, dst, sends, recvs, device):
+        copy = pltpu.make_async_remote_copy(
+            src_ref=src,
+            dst_ref=dst,
+            send_sem=sends,
+            recv_sem=recvs,
+            device_id=device,
+            device_id_type=MESH,
+        )
+        copy.start()
+        pending.append(copy)
+
+    def arrived(ref, sem):
+        pltpu.make_async_copy(ref, ref, sem).wait()
+
+    def weigh(off):
+        zt = (me_z + off) % zs
+        both = jnp.dot(p_ref[zt], d_ref[...], preferred_element_type=jnp.float32)
+        for y in range(ys):
+            part = both[y * LANES : (y + 1) * LANES]
+            num1_ref[zt, y, 0:64, :] = part[0:64, 0:128]
+            num1_ref[zt, y, 64:72, :] = part[:, 128:136].T
+            num2_ref[zt, y, :, :] = part[64:128, 0:128]
+
+    def y_first(off):
+        i = offsets.index(off)
+        zt = (me_z + off) % zs
+        for step in y_steps:
+            send(
+                num1_ref.at[zt, (me_y + step) % ys],
+                ry1_ref.at[step - 1, i],
+                y1_sem.at[0, step - 1, i],
+                y1_sem.at[1, step - 1, i],
+                peer_y(step),
+            )
+
+    def y_merge(off):
+        i = offsets.index(off)
+        zt = (me_z + off) % zs
+        for step in y_steps:
+            arrived(ry1_ref.at[step - 1, i], y1_sem.at[1, step - 1, i])
+        total = num1_ref[zt, me_y]
+        for step in range(1, ys):
+            total = total + ry1_ref[step - 1, i]
+        num1_ref[zt, me_y] = total
+        if off:
+            send(num1_ref.at[zt, me_y], rz1_ref.at[i], z1_sem.at[0, i], z1_sem.at[1, i], peer_z(off))
+
+    def z_send(k, way, chunks):
+        zt = (me_z + (k if way == 0 else zs - k)) % zs
+        for y in chunks:
+            send(
+                num2_ref.at[zt, y],
+                rz2_ref.at[way, k - 1, y],
+                z2_sem.at[0, way, k - 1, y],
+                z2_sem.at[1, way, k - 1, y],
+                peer_z(1 if way == 0 else zs - 1),
+            )
+
+    def z_merge(k, way, chunks):
+        zt = (me_z + (k if way == 0 else zs - k)) % zs
+        for y in chunks:
+            arrived(rz2_ref.at[way, k, y], z2_sem.at[1, way, k, y])
+            num2_ref[zt, y] = num2_ref[zt, y] + rz2_ref[way, k, y]
+
+    every = list(range(ys))
+    parts = [every[: ys // 2], every[ys // 2 :]]
+
+    def z_step(k, merged):
+        for way in range(2):
+            z_merge(k, way, merged[way])
+            z_send(k, way, merged[way])
+
+    weigh(h)
+    z_send(h, 0, parts[0])
+    z_send(h, 1, parts[1])
+    y_first(h)
+    queue = offsets[1:]
+    for _ in range(min(2, len(queue) - 1)):
+        off = queue.pop(0)
+        weigh(off)
+        if h > 1:
+            z_send(h - 1, 0 if off == h - 1 else 1, parts[1] if off == h - 1 else parts[0])
+        y_first(off)
+    for n, off in enumerate(queue):
+        weigh(off)
+        y_first(off)
+        if n == 2 and h > 1:
+            z_step(h - 1, parts)
+    if len(queue) < 3 and h > 1:
+        z_step(h - 1, parts)
+    waiting = list(offsets)
+    for k in range(h - 2, 0, -1):
+        for _ in range(2):
+            y_merge(waiting.pop(0))
+        z_step(k, [every, every])
+    while len(waiting) > 2:
+        y_merge(waiting.pop(0))
+    if h > 0:
+        z_merge(0, 0, every if h > 1 else parts[0])
+        z_merge(0, 1, every if h > 1 else parts[1])
+    for step in y_steps:
+        send(
+            num2_ref.at[me_z, (me_y + step) % ys],
+            ry2_ref.at[step - 1],
+            y2_sem.at[0, step - 1],
+            y2_sem.at[1, step - 1],
+            peer_y(step),
+        )
+    while waiting:
+        y_merge(waiting.pop(0))
+    mine = num1_ref[me_z, me_y]
+    for i in range(zs - 1):
+        arrived(rz1_ref.at[i], z1_sem.at[1, i])
+        mine = mine + rz1_ref[i]
     den = (mine[64:72]).T
     den = den[:, 0:1] + den[:, 1:2]
     targets_ref[0:64, :] = mine[0:64] / den[0:64]
-    targets_ref[64:128, :] = num2_ref[me_z, me_y] / den[64:128]
+    rest = num2_ref[me_z, me_y]
+    for step in y_steps:
+        arrived(ry2_ref.at[step - 1], y2_sem.at[1, step - 1])
+    for step in range(1, ys):
+        rest = rest + ry2_ref[step - 1]
+    targets_ref[64:128, :] = rest / den[64:128]
+    for copy in pending:
+        copy.wait_send()
 
 
 def shards(noise_latents, data_latents, projection):
@@ -434,9 +488,9 @@
         scratch_shapes=[
             pltpu.VMEM((rows, 256), bf16),
             pltpu.VMEM((cols, 256), bf16),
-            pltpu.VMEM((rows, cols), bf16),
+            pltpu.VMEM((zs, ys * LANES, cols), bf16),
             pltpu.VMEM((cols, 256), bf16),
-            pltpu.VMEM((width, 2 * kdim), bf16),
+            pltpu.VMEM((2 * kdim, width), bf16),
             pltpu.VMEM((rch, LANES), f32),
             pltpu.VMEM((cch, LANES), f32),
             pltpu.VMEM((n_noise, 2, cch, LANES), f32),
@@ -444,12 +498,12 @@
             pltpu.VMEM((n_dp, 2, LANES), f32),
             pltpu.VMEM((n_dp, 1, LANES), f32),
             pltpu.VMEM((n_noise, cch, LANES), f32),
-            pltpu.VMEM((ys, zs, 72, LANES), f32),
+            pltpu.VMEM((zs, ys, 72, LANES), f32),
             pltpu.VMEM((zs, ys, 64, LANES), f32),
-            pltpu.VMEM((ys, zs, 72, LANES), f32),
-            pltpu.VMEM((zs, 72, LANES), f32),
-            pltpu.VMEM((zs, ys, 64, LANES), f32),
-            pltpu.VMEM((ys, 64, LANES), f32),
+            pltpu.VMEM((ys - 1, zs, 72, LANES), f32),
+            pltpu.VMEM((zs - 1, 72, LANES), f32),
+            pltpu.VMEM((2, zs // 2, ys, 64, LANES), f32),
+            pltpu.VMEM((ys - 1, 64, LANES), f32),
             dma((n_noise,)),
             dma((n_noise,)),
             dma((n_dp,)),
@@ -458,10 +512,10 @@
             dma((n_dp,)),
             dma((n_noise,)),
             dma((n_noise,)),
-            dma((2, ys // 2, 2)),
-            dma((2, zs // 2, 2)),
-            dma((2, zs // 2, 2)),
-            dma((2, ys // 2, 2)),
+            dma((2, ys - 1, zs)),
+            dma((2, zs - 1)),
+            dma((2, 2, zs // 2, ys)),
+            dma((2, ys - 1)),
         ],
         compiler_params=pltpu.CompilerParams(
             collective_id=0, has_side_effects=True, vmem_limit_bytes=56 * 2**20
@@ -469,7 +523,7 @@
         cost_estimate=pl.CostEstimate(
             flops=8 * rows * cols * 256, bytes_accessed=2**21, transcendentals=3 * rows * cols
         ),
-    )(noise_latents, data_latents, projection)
+    )(noise_latents, data_latents, projection.T)
     return (targets, pot.reshape(cols))
 
 

time: 104 us -> 89.6 us (0.86)
  the two profiles are of different devices: /device:TPU:4 before, /device:TPU:1 now
where the time goes in v2:
time: 89.6 us; the launch traced here: 88.4 us
  Pallas kernels  85.7 us (96%)
  local copies, waits for them, and re-layouts  2.08 us (2%)
    pallas_call x1, Pallas kernels, shards(): pl.pallas_call(functools.partial(kernel, cfg), out_shape=(jax.ShapeDtypeS...  85.7 us
    unnamed x4, local copies, waits for them, and re-layouts  2.08 us

profile of v2, /device:TPU:1, one launch (start us, length us, event | category | flops | bytes accessed | tf_op | source)
XLA Modules:
  0.0 88.4 jit_solution(3135431829591882074)
XLA Ops:
  0.6 85.7 %shard_map.50 = (f32[128,128]{1,0:T(8,128)}, f32[16,128]{1,0:T(8,128)}) custom-call(bf16[4096,128]{1,0:T(8,128)(2,1)} %noise_ref.1, bf16[2048,128]{1,0:T(8,128)(2,1)} %data_ref.1, bf16[64,128]{1,0:T(8,128)(2,1)} %bitcast.3), custom_call_target="tpu_custom_call" | custom-call | flops 17179869184 | bytes 2097152 | tf_op jit(solution)/shard_map/pallas_call | solution.py:480
  86.3 0.0 copy-start
  86.4 1.5 %copy.7 = f32[128,128]{1,0:T(8,128)} copy(f32[128,128]{1,0:T(8,128)} %get-tuple-element.8) | data formatting | bytes 131072
  87.8 0.0 copy-done
  87.8 0.6 copy.8
Async XLA Ops:
  86.3 1.5 %copy-start = (f32[16,128]{1,0:T(8,128)S(1)}, f32[16,128]{1,0:T(8,128)}, u32[]{:S(2)}) copy-start(f32[16,128]{1,0:T(8,128)} %get-tuple-element.5) | copy-start | bytes 24580

commit v3 on v2

v3 whole, which is shorter than its diff:
```python
import functools
import math

import jax
import jax.numpy as jnp
from jax import lax
from jax.experimental import pallas as pl
from jax.experimental.pallas import tpu as pltpu
from jax.sharding import PartitionSpec as P

epsilon = 0.02
LOG2E = 1.0 / math.log(2.0)
LN2 = math.log(2.0)
NT = (((1,), (1,)), ((), ()))
MESH = pl.DeviceIdType.MESH
LANES = 128


def ring_sizes(dp):
    return {32: (4, 8), 8: (2, 4), 16: (4, 4)}[dp]


def split3(x):
    hi = x.astype(jnp.bfloat16).astype(jnp.float32)
    rest = x - hi
    mid = rest.astype(jnp.bfloat16).astype(jnp.float32)
    return hi, mid, rest - mid


def kernel(
    cfg,
    noise_ref,
    data_ref,
    proj_ref,
    targets_ref,
    pot_ref,
    q_ref,
    r_ref,
    p_ref,
    d_ref,
    proj2_ref,
    ul_ref,
    vl_ref,
    st1_ref,
    lse_ref,
    rho_ref,
    gy1_ref,
    gz1_ref,
    gz2_ref,
    gy2_ref,
    st3_ref,
    num_ref,
    far_ref,
    near_ref,
    rz_ref,
    s1_sem,
    s3_sem,
    gy1_sem,
    gz1_sem,
    gz2_sem,
    gy2_sem,
    far_sem,
    near_sem,
    rz_sem,
):
    rows, cols, n_noise, n_dp, kdim = cfg
    ys, zs = ring_sizes(n_dp)
    rch, cch = rows // LANES, cols // LANES
    log_rows = math.log2(rows * n_noise)
    log_cols = math.log2(cols * n_dp)
    scale = 2.0 * LOG2E / (kdim * epsilon)
    norm_scale = LOG2E / (kdim * epsilon)
    me_n = lax.axis_index("noise")
    me_d = lax.axis_index("dp")
    me_y, me_z = me_d // zs, me_d % zs

    def peer_noise(step):
        return ((me_n + step) % n_noise, me_d)

    def peer_y(step):
        return (me_n, (me_y + step) % ys * zs + me_z)

    def peer_z(step):
        return (me_n, me_y * zs + (me_z + step) % zs)

    barrier = pltpu.get_barrier_semaphore()

    def greet_noise(k, carry):
        pl.semaphore_signal(barrier, inc=1, device_id=peer_noise(k), device_id_type=MESH)
        return carry

    def greet_y(k, carry):
        pl.semaphore_signal(barrier, inc=1, device_id=peer_y(k), device_id_type=MESH)
        return carry

    def greet_z(k, carry):
        pl.semaphore_signal(barrier, inc=1, device_id=peer_z(k), device_id_type=MESH)
        return carry

    lax.fori_loop(1, n_noise, greet_noise, 0)
    lax.fori_loop(1, ys, greet_y, 0)
    lax.fori_loop(1, zs, greet_z, 0)

    proj2_ref[0:kdim, :] = proj_ref[...]
    proj2_ref[kdim : 2 * kdim, :] = proj_ref[...]
    half = jnp.full((8, LANES), 0.5, jnp.bfloat16)
    one = jnp.ones((1, LANES), jnp.float32)
    zero = jnp.zeros((2, LANES), jnp.float32)

    def put_bias(dst_ref, c, bias, first):
        parts = list(split3(bias))
        ones = [one, one, one]
        tile = jnp.concatenate((parts + ones if first else ones + parts) + [zero], axis=0)
        dst_ref[c * LANES : (c + 1) * LANES, 128:136] = tile.T.astype(jnp.bfloat16)

    def prepare(src_ref, dst_ref, bias_ref, count, is_q):
        step = min(512, count)

        def body(b, carry):
            sl = pl.ds(pl.multiple_of(b * step, step), step)
            proj = lax.dot_general(
                src_ref[sl, :], proj2_ref[...], NT, preferred_element_type=jnp.float32
            )
            code = proj.astype(jnp.bfloat16)
            full = code.astype(jnp.float32)
            square = full * full
            sq_hi = square.astype(jnp.bfloat16)
            sq_lo = (square - sq_hi.astype(jnp.float32)).astype(jnp.bfloat16)
            norm = lax.dot_general(
                half, sq_hi, NT, preferred_element_type=jnp.float32
            ) + lax.dot_general(half, sq_lo, NT, preferred_element_type=jnp.float32)
            if is_q:
                dst_ref[sl, 0:128] = code
            else:
                scaled = full * scale
                hi = scaled.astype(jnp.bfloat16)
                lo = (scaled - hi.astype(jnp.float32)).astype(jnp.bfloat16)
                lane = lax.broadcasted_iota(jnp.int32, scaled.shape, 1)
                dst_ref[sl, 0:128] = jnp.where(
                    lane < kdim, hi.astype(jnp.float32), lo.astype(jnp.float32)
                ).astype(jnp.bfloat16)
            dst_ref[sl, 128:256] = jnp.zeros((step, 128), jnp.bfloat16)
            for c in range(step // LANES):
                bias_ref[pl.ds(b * (step // LANES) + c, 1), :] = (
                    -norm_scale * norm[0:1, c * LANES : (c + 1) * LANES]
                )
            return carry

        lax.fori_loop(0, count // step, body, 0)
        bias = bias_ref[...]
        for c in range(count // LANES):
            put_bias(dst_ref, c, bias[c : c + 1, :], is_q)

    prepare(noise_ref, q_ref, ul_ref, rows, True)
    prepare(data_ref, r_ref, vl_ref, cols, False)

    def lse_pass(lhs_ref, count, rhs_ref, width, write):
        bw = min(2048, width)
        bl = 256
        un = min(4, count // bl)

        def wide(w, carry):
            rhs = rhs_ref[pl.ds(pl.multiple_of(w * bw, bw), bw), :]

            def body(step, state):
                top, total = state
                for u in range(un):
                    sl = pl.ds(pl.multiple_of((step * un + u) * bl, bl), bl)
                    z = lax.dot_general(
                        lhs_ref[sl, :], rhs, NT, preferred_element_type=jnp.float32
                    ).reshape(bl // 8, 8, bw)
                    new = jnp.maximum(top, jnp.max(z, axis=0))
                    total = total * jnp.exp2(top - new) + jnp.sum(jnp.exp2(z - new[None]), axis=0)
                    top = new
                return top, total

            start = (jnp.full((8, bw), -1e30, jnp.float32), jnp.zeros((8, bw), jnp.float32))
            top, total = lax.fori_loop(0, count // (bl * un), body, start)
            best = jnp.max(top, axis=0, keepdims=True)
            write(w, bw, best, jnp.sum(total * jnp.exp2(top - best), axis=0, keepdims=True))
            return carry

        lax.fori_loop(0, width // bw, wide, 0)

    def gather(ref, sem, size, me, peer):
        def copy(k):
            return pltpu.make_async_remote_copy(
                src_ref=ref.at[me],
                dst_ref=ref.at[me],
                send_sem=sem.at[0, k],
                recv_sem=sem.at[1, me],
                device_id=peer(k),
                device_id_type=MESH,
            )

        def start(k, carry):
            copy(k).start()
            return carry

        def wait(k, carry):
            source = (me + size - k) % size
            pltpu.make_async_copy(ref.at[source], ref.at[source], sem.at[1, source]).wait()
            copy(k).wait_send()
            return carry

        lax.fori_loop(1, size, start, 0)
        return lambda: lax.fori_loop(1, size, wait, 0)

    def joined(ref, size):
        top = ref[0]
        for k in range(1, size):
            top = jnp.maximum(top, ref[k])
        total = jnp.exp2(ref[0] - top)
        for k in range(1, size):
            total = total + jnp.exp2(ref[k] - top)
        return top + jnp.log(total) * LOG2E

    def write1(w, bw, top, total):
        lse = top + jnp.log(total) * LOG2E
        for c in range(bw // LANES):
            put = pl.ds(w * (bw // LANES) + c, 1)
            st1_ref[me_n, put, :] = lse[:, c * LANES : (c + 1) * LANES]

    def write2(w, bw, top, total):
        lse = top + jnp.log(total) * LOG2E
        for c in range(bw // LANES):
            put = pl.ds(w * (bw // LANES) + c, 1)
            lse_ref[put, :] = lse[:, c * LANES : (c + 1) * LANES]

    lse_pass(q_ref, rows, r_ref, cols, write1)
    pl.semaphore_wait(barrier, n_noise - 1 + ys - 1 + zs - 1)

    gather(st1_ref, s1_sem, n_noise, me_n, peer_noise)()
    g1 = log_rows - joined(st1_ref, n_noise)
    vl = vl_ref[...] + g1
    for c in range(cch):
        put_bias(r_ref, c, vl[c : c + 1, :], False)

    lse_pass(r_ref, cols, q_ref, rows, write2)

    bl, bw, un = 256, cols, min(4, rows // 256)
    per = bl // LANES

    def weights(step, carry):
        for u in range(un):
            tile = step * un + u
            sl = pl.ds(pl.multiple_of(tile * bl, bl), bl)
            z = lax.dot_general(q_ref[sl, :], r_ref[...], NT, preferred_element_type=jnp.float32)
            p = jnp.exp2(z).astype(jnp.bfloat16)
            for i in range(per):
                chunk = tile * per + i
                put = pl.ds(pl.multiple_of(chunk // zs * LANES, LANES), LANES)
                p_ref[chunk % zs, put, :] = p[i * LANES : (i + 1) * LANES]
        return carry

    hch = rch // 2
    steps = rows // (bl * un)
    gy1_ref[me_y] = lse_ref[0:hch]
    gz2_ref[me_z] = lse_ref[hch:rch]
    wait_y = gather(gy1_ref, gy1_sem, ys, me_y, peer_y)
    wait_z = gather(gz2_ref, gz2_sem, zs, me_z, peer_z)
    lse = lse_ref[...]
    ul = ul_ref[...] - lse
    for c in range(rch):
        put_bias(q_ref, c, ul[c : c + 1, :], True)
    lax.fori_loop(0, steps // 2, weights, 0)
    wait_y()
    gz1_ref[me_z] = joined(gy1_ref, ys)
    wait_y = gather(gz1_ref, gz1_sem, zs, me_z, peer_z)
    wait_z()
    gy2_ref[me_y] = joined(gz2_ref, zs)
    wait_z = gather(gy2_ref, gy2_sem, ys, me_y, peer_y)
    lax.fori_loop(steps // 2, steps, weights, 0)
    wait_y()
    rho_ref[0:hch] = jnp.exp2(lse[0:hch] - joined(gz1_ref, zs) + log_cols)
    wait_z()
    rho_ref[hch:rch] = jnp.exp2(lse[hch:rch] - joined(gy2_ref, ys) + log_cols)

    rho = rho_ref[...]
    rho_hi = rho.astype(jnp.bfloat16).astype(jnp.float32)
    rho_lo = rho - rho_hi
    zero6 = jnp.zeros((6, ys * LANES), jnp.float32)
    total = jnp.zeros((8, cols), jnp.float32)
    for z in range(zs):
        lines = []
        for part in (rho_hi, rho_lo):
            lines.append(
                jnp.concatenate([part[y * zs + z : y * zs + z + 1] for y in range(ys)], axis=1)
            )
        lhs = jnp.concatenate(lines + [zero6], axis=0).astype(jnp.bfloat16)
        total = total + jnp.dot(lhs, p_ref[z], preferred_element_type=jnp.float32)
    total = total[0:1] + total[1:2]
    for c in range(cch):
        st3_ref[me_n, c : c + 1, :] = total[:, c * LANES : (c + 1) * LANES]
    gather(st3_ref, s3_sem, n_noise, me_n, peer_noise)()
    total = st3_ref[0]
    for k in range(1, n_noise):
        total = total + st3_ref[k]
    pot_ref[...] = (epsilon * LN2) * (g1 + log_rows - jnp.log(total) * LOG2E)

    factor = float(rows * n_noise) / total
    f_hi = factor.astype(jnp.bfloat16).astype(jnp.float32)
    f_lo = factor - f_hi
    zero5 = jnp.zeros((5, LANES), jnp.float32)
    for c in range(cch):
        sl = slice(c * LANES, (c + 1) * LANES)
        tile = jnp.concatenate(
            [f_hi[c : c + 1], f_lo[c : c + 1], factor[c : c + 1], zero5], axis=0
        ).T
        d_ref[sl, 0:128] = (data_ref[sl, :].astype(jnp.float32) * tile[:, 2:3]).astype(
            jnp.bfloat16
        )
        d_ref[sl, 128:256] = jnp.zeros((LANES, 128), jnp.bfloat16)
        d_ref[sl, 128:136] = tile.astype(jnp.bfloat16)

    h = zs // 2
    offsets = [h]
    for k in range(h - 1, 0, -1):
        offsets += [k, zs - k]
    offsets.append(0)
    pending = []
    cuts = (pl.ds(0, 72), pl.ds(72, 64))

    def send(src, dst, sem, device):
        copy = pltpu.make_async_remote_copy(
            src_ref=src,
            dst_ref=dst,
            send_sem=sem.at[0],
            recv_sem=sem.at[1],
            device_id=device,
            device_id_type=MESH,
        )
        copy.start()
        pending.append(copy)

    def arrived(ref, sem):
        pltpu.make_async_copy(ref, ref, sem.at[1]).wait()

    def weigh(off):
        zt = (me_z + off) % zs
        both = jnp.dot(p_ref[zt], d_ref[...], preferred_element_type=jnp.float32)
        for y in range(ys):
            line = rho_ref[pl.ds(y * zs + zt, 1), :]
            column = jnp.broadcast_to(line, (8, LANES)).T[:, 0:1]
            part = both[y * LANES : (y + 1) * LANES] * column
            num_ref[zt, y, 0:64, :] = part[0:64, 0:128]
            num_ref[zt, y, 64:72, :] = part[:, 128:136].T
            num_ref[zt, y, 72:136, :] = part[64:128, 0:128]

    def along(way, step):
        return (me_y + (step if way == 0 else ys - step)) % ys

    def y_send(i):
        zt = (me_z + offsets[i]) % zs
        if ys == 4:
            for way in range(2):
                send(
                    num_ref.at[zt, along(way, 2), cuts[way]],
                    far_ref.at[i, cuts[way]],
                    far_sem.at[i, way],
                    peer_y(1 if way == 0 else ys - 1),
                )
        for way in range(2):
            send(
                num_ref.at[zt, along(way, 1), cuts[1 - way]],
                near_ref.at[way, i, cuts[1 - way]],
                near_sem.at[way, i, 0],
                peer_y(1 if way == 0 else ys - 1),
            )

    def y_forward(i):
        if ys != 4:
            return
        zt = (me_z + offsets[i]) % zs
        for way in range(2):
            arrived(far_ref.at[i, cuts[way]], far_sem.at[i, way])
            to = along(way, 1)
            num_ref[zt, to, cuts[way]] = num_ref[zt, to, cuts[way]] + far_ref[i, cuts[way]]
            send(
                num_ref.at[zt, to, cuts[way]],
                near_ref.at[way, i, cuts[way]],
                near_sem.at[way, i, 1],
                peer_y(1 if way == 0 else ys - 1),
            )

    def y_merge(i):
        zt = (me_z + offsets[i]) % zs
        for way in range(2):
            arrived(near_ref.at[way, i, cuts[1 - way]], near_sem.at[way, i, 0])
            if ys == 4:
                arrived(near_ref.at[way, i, cuts[way]], near_sem.at[way, i, 1])
        if ys == 4:
            num_ref[zt, me_y] = num_ref[zt, me_y] + near_ref[0, i] + near_ref[1, i]
        else:
            for way in range(2):
                part = cuts[1 - way]
                num_ref[zt, me_y, part] = num_ref[zt, me_y, part] + near_ref[way, i, part]
        if offsets[i]:
            send(num_ref.at[zt, me_y], rz_ref.at[i], rz_sem.at[i], peer_z(offsets[i]))

    lag = zs // 2
    for i in range(zs):
        weigh(offsets[i])
        y_send(i)
        if i >= lag:
            y_forward(i - lag)
    for i in range(lag):
        y_forward(zs - lag + i)
        y_merge(i)
    for i in range(lag, zs):
        y_merge(i)
    mine = num_ref[me_z, me_y]
    for i in range(zs - 1):
        arrived(rz_ref.at[i], rz_sem.at[i])
        mine = mine + rz_ref[i]
    den = (mine[64:72]).T
    den = den[:, 0:1] + den[:, 1:2]
    targets_ref[0:64, :] = mine[0:64] / den[0:64]
    targets_ref[64:128, :] = mine[72:136] / den[64:128]
    for copy in pending:
        copy.wait_send()


def shards(noise_latents, data_latents, projection):
    rows, width = noise_latents.shape
    cols = data_latents.shape[0]
    kdim = projection.shape[1]
    n_noise, n_dp = lax.axis_size("noise"), lax.axis_size("dp")
    ys, zs = ring_sizes(n_dp)
    rch, cch = rows // LANES, cols // LANES
    f32, bf16 = jnp.float32, jnp.bfloat16
    cfg = (rows, cols, n_noise, n_dp, kdim)
    dma = pltpu.SemaphoreType.DMA
    vmem = pl.BlockSpec(memory_space=pltpu.VMEM)
    targets, pot = pl.pallas_call(
        functools.partial(kernel, cfg),
        out_shape=(
            jax.ShapeDtypeStruct((LANES, width), f32),
            jax.ShapeDtypeStruct((cch, LANES), f32),
        ),
        in_specs=[vmem] * 3,
        out_specs=(vmem, vmem),
        scratch_shapes=[
            pltpu.VMEM((rows, 256), bf16),
            pltpu.VMEM((cols, 256), bf16),
            pltpu.VMEM((zs, ys * LANES, cols), bf16),
            pltpu.VMEM((cols, 256), bf16),
            pltpu.VMEM((2 * kdim, width), bf16),
            pltpu.VMEM((rch, LANES), f32),
            pltpu.VMEM((cch, LANES), f32),
            pltpu.VMEM((n_noise, cch, LANES), f32),
            pltpu.VMEM((rch, LANES), f32),
            pltpu.VMEM((rch, LANES), f32),
            pltpu.VMEM((ys, rch // 2, LANES), f32),
            pltpu.VMEM((zs, rch // 2, LANES), f32),
            pltpu.VMEM((zs, rch // 2, LANES), f32),
            pltpu.VMEM((ys, rch // 2, LANES), f32),
            pltpu.VMEM((n_noise, cch, LANES), f32),
            pltpu.VMEM((zs, ys, 136, LANES), f32),
            pltpu.VMEM((zs, 136, LANES), f32),
            pltpu.VMEM((2, zs, 136, LANES), f32),
            pltpu.VMEM((zs - 1, 136, LANES), f32),
            dma((2, n_noise)),
            dma((2, n_noise)),
            dma((2, ys)),
            dma((2, zs)),
            dma((2, zs)),
            dma((2, ys)),
            dma((zs, 2, 2)),
            dma((2, zs, 2, 2)),
            dma((zs - 1, 2)),
        ],
        compiler_params=pltpu.CompilerParams(
            collective_id=0, has_side_effects=True, vmem_limit_bytes=56 * 2**20
        ),
        cost_estimate=pl.CostEstimate(
            flops=8 * rows * cols * 256, bytes_accessed=2**21, transcendentals=3 * rows * cols
        ),
    )(noise_latents, data_latents, projection.T)
    return (targets, pot.reshape(cols))


def solution(mesh):
    in_specs = (P("noise", None), P("dp", None), P())
    out_specs = (P(("noise", "dp"), None), P("dp"))
    return jax.shard_map(shards, mesh=mesh, in_specs=in_specs, out_specs=out_specs, check_vma=False)
```

time: 89.6 us -> 80.9 us (0.903); the launches traced: 88.4 us -> 80.8 us
  Pallas kernels: 85.7 us -> 78.1 us
    pallas_call x1, Pallas kernels: 85.7 us -> 78.1 us  [shards(): pl.pallas_call(functools.partial(kernel, cfg), out_shape=(jax.ShapeDtypeS...]
where the time goes in v3:
time: 80.9 us; the launch traced here: 80.8 us
  Pallas kernels  78.1 us (97%)
  local copies, waits for them, and re-layouts  2.08 us (3%)
    pallas_call x1, Pallas kernels, shards(): pl.pallas_call(functools.partial(kernel, cfg), out_shape=(jax.ShapeDtypeS...  78.1 us
    unnamed x4, local copies, waits for them, and re-layouts  2.08 us

profile of v3, /device:TPU:1, one launch (start us, length us, event | category | flops | bytes accessed | tf_op | source)
XLA Modules:
  0.0 80.8 jit_solution(13396014089934985074)
XLA Ops:
  0.6 78.1 %shard_map.50 = (f32[128,128]{1,0:T(8,128)}, f32[16,128]{1,0:T(8,128)}) custom-call(bf16[4096,128]{1,0:T(8,128)(2,1)} %noise_ref.1, bf16[2048,128]{1,0:T(8,128)(2,1)} %data_ref.1, bf16[64,128]{1,0:T(8,128)(2,1)} %bitcast.3), custom_call_target="tpu_custom_call" | custom-call | flops 17179869184 | bytes 2097152 | tf_op jit(solution)/shard_map/pallas_call | solution.py:435
  78.7 0.0 copy-start
  78.7 1.5 %copy.7 = f32[128,128]{1,0:T(8,128)} copy(f32[128,128]{1,0:T(8,128)} %get-tuple-element.8) | data formatting | bytes 131072
  80.2 0.0 copy-done
  80.2 0.6 copy.8
Async XLA Ops:
  78.7 1.5 %copy-start = (f32[16,128]{1,0:T(8,128)S(1)}, f32[16,128]{1,0:T(8,128)}, u32[]{:S(2)}) copy-start(f32[16,128]{1,0:T(8,128)} %get-tuple-element.5) | copy-start | bytes 24580

commit v4 on v3

--- a/solution.py
+++ b/solution.py
@@ -41,13 +41,13 @@
     proj2_ref,
     ul_ref,
     vl_ref,
-    st1_ref,
-    lse_ref,
+    st1a_ref,
+    st1b_ref,
+    lsea_ref,
+    lseb_ref,
     rho_ref,
-    gy1_ref,
-    gz1_ref,
-    gz2_ref,
-    gy2_ref,
+    gy_ref,
+    gz_ref,
     st3_ref,
     num_ref,
     far_ref,
@@ -55,10 +55,8 @@
     rz_ref,
     s1_sem,
     s3_sem,
-    gy1_sem,
-    gz1_sem,
-    gz2_sem,
-    gy2_sem,
+    gy_sem,
+    gz_sem,
     far_sem,
     near_sem,
     rz_sem,
@@ -114,7 +112,7 @@
         dst_ref[c * LANES : (c + 1) * LANES, 128:136] = tile.T.astype(jnp.bfloat16)
 
     def prepare(src_ref, dst_ref, bias_ref, count, is_q):
-        step = min(512, count)
+        step = min(2048, count)
 
         def body(b, carry):
             sl = pl.ds(pl.multiple_of(b * step, step), step)
@@ -154,18 +152,18 @@
     prepare(noise_ref, q_ref, ul_ref, rows, True)
     prepare(data_ref, r_ref, vl_ref, cols, False)
 
-    def lse_pass(lhs_ref, count, rhs_ref, width, write):
+    def lse_pass(lhs_ref, first, count, rhs_ref, start, width, write):
         bw = min(2048, width)
         bl = 256
-        un = min(4, count // bl)
+        un = max(1, min(2**21 // (bl * bw), count // bl))
 
         def wide(w, carry):
-            rhs = rhs_ref[pl.ds(pl.multiple_of(w * bw, bw), bw), :]
+            rhs = rhs_ref[pl.ds(pl.multiple_of(start + w * bw, bw), bw), :]
 
             def body(step, state):
                 top, total = state
                 for u in range(un):
-                    sl = pl.ds(pl.multiple_of((step * un + u) * bl, bl), bl)
+                    sl = pl.ds(pl.multiple_of(first + (step * un + u) * bl, bl), bl)
                     z = lax.dot_general(
                         lhs_ref[sl, :], rhs, NT, preferred_element_type=jnp.float32
                     ).reshape(bl // 8, 8, bw)
@@ -174,10 +172,13 @@
                     top = new
                 return top, total
 
-            start = (jnp.full((8, bw), -1e30, jnp.float32), jnp.zeros((8, bw), jnp.float32))
-            top, total = lax.fori_loop(0, count // (bl * un), body, start)
+            state = (jnp.full((8, bw), -1e30, jnp.float32), jnp.zeros((8, bw), jnp.float32))
+            top, total = lax.fori_loop(0, count // (bl * un), body, state)
             best = jnp.max(top, axis=0, keepdims=True)
-            write(w, bw, best, jnp.sum(total * jnp.exp2(top - best), axis=0, keepdims=True))
+            total = jnp.sum(total * jnp.exp2(top - best), axis=0, keepdims=True)
+            lse = best + jnp.log(total) * LOG2E
+            for c in range(bw // LANES):
+                write(w * (bw // LANES) + c, lse[:, c * LANES : (c + 1) * LANES])
             return carry
 
         lax.fori_loop(0, width // bw, wide, 0)
@@ -215,28 +216,29 @@
             total = total + jnp.exp2(ref[k] - top)
         return top + jnp.log(total) * LOG2E
 
-    def write1(w, bw, top, total):
-        lse = top + jnp.log(total) * LOG2E
-        for c in range(bw // LANES):
-            put = pl.ds(w * (bw // LANES) + c, 1)
-            st1_ref[me_n, put, :] = lse[:, c * LANES : (c + 1) * LANES]
-
-    def write2(w, bw, top, total):
-        lse = top + jnp.log(total) * LOG2E
-        for c in range(bw // LANES):
-            put = pl.ds(w * (bw // LANES) + c, 1)
-            lse_ref[put, :] = lse[:, c * LANES : (c + 1) * LANES]
-
-    lse_pass(q_ref, rows, r_ref, cols, write1)
-    pl.semaphore_wait(barrier, n_noise - 1 + ys - 1 + zs - 1)
-
-    gather(st1_ref, s1_sem, n_noise, me_n, peer_noise)()
-    g1 = log_rows - joined(st1_ref, n_noise)
-    vl = vl_ref[...] + g1
-    for c in range(cch):
-        put_bias(r_ref, c, vl[c : c + 1, :], False)
-
-    lse_pass(r_ref, cols, q_ref, rows, write2)
+    hcol, hch = cols // 2, cch // 2
+    waits, g1 = [], []
+    for i, ref in enumerate((st1a_ref, st1b_ref)):
+
+        def write(chunk, line):
+            ref[me_n, pl.ds(chunk, 1), :] = line
+
+        lse_pass(q_ref, 0, rows, r_ref, i * hcol, hcol, write)
+        if i == 0:
+            pl.semaphore_wait(barrier, n_noise - 1 + ys - 1 + zs - 1)
+        waits.append(gather(ref, s1_sem.at[i], n_noise, me_n, peer_noise))
+    for i, (ref, out_ref) in enumerate(((st1a_ref, lsea_ref), (st1b_ref, lseb_ref))):
+        waits[i]()
+        g1.append(log_rows - joined(ref, n_noise))
+        vl = vl_ref[i * hch : (i + 1) * hch] + g1[i]
+        for c in range(hch):
+            put_bias(r_ref, i * hch + c, vl[c : c + 1, :], False)
+
+        def write(chunk, line):
+            out_ref[pl.ds(chunk, 1), :] = line
+
+        lse_pass(r_ref, i * hcol, hcol, q_ref, 0, rows, write)
+    g1 = jnp.concatenate(g1, axis=0)
 
     bl, bw, un = 256, cols, min(4, rows // 256)
     per = bl // LANES
@@ -253,28 +255,21 @@
                 p_ref[chunk % zs, put, :] = p[i * LANES : (i + 1) * LANES]
         return carry
 
-    hch = rch // 2
     steps = rows // (bl * un)
-    gy1_ref[me_y] = lse_ref[0:hch]
-    gz2_ref[me_z] = lse_ref[hch:rch]
-    wait_y = gather(gy1_ref, gy1_sem, ys, me_y, peer_y)
-    wait_z = gather(gz2_ref, gz2_sem, zs, me_z, peer_z)
-    lse = lse_ref[...]
+    top = jnp.maximum(lsea_ref[...], lseb_ref[...])
+    lse = top + LOG2E * jnp.log(jnp.exp2(lsea_ref[...] - top) + jnp.exp2(lseb_ref[...] - top))
+    gy_ref[me_y] = lse
+    wait = gather(gy_ref, gy_sem, ys, me_y, peer_y)
     ul = ul_ref[...] - lse
     for c in range(rch):
         put_bias(q_ref, c, ul[c : c + 1, :], True)
     lax.fori_loop(0, steps // 2, weights, 0)
-    wait_y()
-    gz1_ref[me_z] = joined(gy1_ref, ys)
-    wait_y = gather(gz1_ref, gz1_sem, zs, me_z, peer_z)
-    wait_z()
-    gy2_ref[me_y] = joined(gz2_ref, zs)
-    wait_z = gather(gy2_ref, gy2_sem, ys, me_y, peer_y)
+    wait()
+    gz_ref[me_z] = joined(gy_ref, ys)
+    wait = gather(gz_ref, gz_sem, zs, me_z, peer_z)
     lax.fori_loop(steps // 2, steps, weights, 0)
-    wait_y()
-    rho_ref[0:hch] = jnp.exp2(lse[0:hch] - joined(gz1_ref, zs) + log_cols)
-    wait_z()
-    rho_ref[hch:rch] = jnp.exp2(lse[hch:rch] - joined(gy2_ref, ys) + log_cols)
+    wait()
+    rho_ref[...] = jnp.exp2(lse - joined(gz_ref, zs) + log_cols)
 
     rho = rho_ref[...]
     rho_hi = rho.astype(jnp.bfloat16).astype(jnp.float32)
@@ -350,7 +345,7 @@
     def along(way, step):
         return (me_y + (step if way == 0 else ys - step)) % ys
 
-    def y_send(i):
+    def y_far(i):
         zt = (me_z + offsets[i]) % zs
         if ys == 4:
             for way in range(2):
@@ -360,6 +355,9 @@
                     far_sem.at[i, way],
                     peer_y(1 if way == 0 else ys - 1),
                 )
+
+    def y_near(i):
+        zt = (me_z + offsets[i]) % zs
         for way in range(2):
             send(
                 num_ref.at[zt, along(way, 1), cuts[1 - way]],
@@ -398,16 +396,13 @@
         if offsets[i]:
             send(num_ref.at[zt, me_y], rz_ref.at[i], rz_sem.at[i], peer_z(offsets[i]))
 
-    lag = zs // 2
     for i in range(zs):
         weigh(offsets[i])
-        y_send(i)
-        if i >= lag:
-            y_forward(i - lag)
-    for i in range(lag):
-        y_forward(zs - lag + i)
-        y_merge(i)
-    for i in range(lag, zs):
+        y_far(i)
+    for i in range(zs):
+        y_near(i)
+        y_forward(i)
+    for i in range(zs):
         y_merge(i)
     mine = num_ref[me_z, me_y]
     for i in range(zs - 1):
@@ -448,24 +443,22 @@
             pltpu.VMEM((2 * kdim, width), bf16),
             pltpu.VMEM((rch, LANES), f32),
             pltpu.VMEM((cch, LANES), f32),
-            pltpu.VMEM((n_noise, cch, LANES), f32),
+            pltpu.VMEM((n_noise, cch // 2, LANES), f32),
+            pltpu.VMEM((n_noise, cch // 2, LANES), f32),
             pltpu.VMEM((rch, LANES), f32),
             pltpu.VMEM((rch, LANES), f32),
-            pltpu.VMEM((ys, rch // 2, LANES), f32),
-            pltpu.VMEM((zs, rch // 2, LANES), f32),
-            pltpu.VMEM((zs, rch // 2, LANES), f32),
-            pltpu.VMEM((ys, rch // 2, LANES), f32),
+            pltpu.VMEM((rch, LANES), f32),
+            pltpu.VMEM((ys, rch, LANES), f32),
+            pltpu.VMEM((zs, rch, LANES), f32),
             pltpu.VMEM((n_noise, cch, LANES), f32),
             pltpu.VMEM((zs, ys, 136, LANES), f32),
             pltpu.VMEM((zs, 136, LANES), f32),
             pltpu.VMEM((2, zs, 136, LANES), f32),
             pltpu.VMEM((zs - 1, 136, LANES), f32),
-            dma((2, n_noise)),
+            dma((2, 2, n_noise)),
             dma((2, n_noise)),
             dma((2, ys)),
             dma((2, zs)),
-            dma((2, zs)),
-            dma((2, ys)),
             dma((zs, 2, 2)),
             dma((2, zs, 2, 2)),
             dma((zs - 1, 2)),

time: 80.9 us -> 77.9 us (0.963)
  Pallas kernels: 78.1 us -> 75 us
    pallas_call x1, Pallas kernels: 78.1 us -> 75 us  [shards(): pl.pallas_call(functools.partial(kernel, cfg), out_shape=(jax.ShapeDtypeS...]
where the time goes in v4:
time: 77.9 us; the launch traced here: 77.7 us
  Pallas kernels  75 us (96%)
  local copies, waits for them, and re-layouts  2.08 us (3%)
    pallas_call x1, Pallas kernels, shards(): pl.pallas_call(functools.partial(kernel, cfg), out_shape=(jax.ShapeDtypeS...  75 us
    unnamed x4, local copies, waits for them, and re-layouts  2.08 us

profile of v4, /device:TPU:1, one launch (start us, length us, event | category | flops | bytes accessed | tf_op | source)
XLA Modules:
  0.0 77.7 jit_solution(16662505335949010502)
XLA Ops:
  0.6 75.0 %shard_map.50 = (f32[128,128]{1,0:T(8,128)}, f32[16,128]{1,0:T(8,128)}) custom-call(bf16[4096,128]{1,0:T(8,128)(2,1)} %noise_ref.1, bf16[2048,128]{1,0:T(8,128)(2,1)} %data_ref.1, bf16[64,128]{1,0:T(8,128)(2,1)} %bitcast.3), custom_call_target="tpu_custom_call" | custom-call | flops 17179869184 | bytes 2097152 | tf_op jit(solution)/shard_map/pallas_call | solution.py:430
  75.6 0.0 copy-start
  75.6 1.5 %copy.7 = f32[128,128]{1,0:T(8,128)} copy(f32[128,128]{1,0:T(8,128)} %get-tuple-element.8) | data formatting | bytes 131072
  77.1 0.0 copy-done
  77.1 0.6 copy.8
Async XLA Ops:
  75.6 1.5 %copy-start = (f32[16,128]{1,0:T(8,128)S(1)}, f32[16,128]{1,0:T(8,128)}, u32[]{:S(2)}) copy-start(f32[16,128]{1,0:T(8,128)} %get-tuple-element.5) | copy-start | bytes 24580

commit v5 on v4

--- a/solution.py
+++ b/solution.py
@@ -45,14 +45,19 @@
     st1b_ref,
     lsea_ref,
     lseb_ref,
+    lse_ref,
     rho_ref,
-    gy_ref,
-    gz_ref,
+    gya_ref,
+    gyb_ref,
+    gza_ref,
+    gzb_ref,
     st3_ref,
     num_ref,
     far_ref,
     near_ref,
     rz_ref,
+    zf_ref,
+    yf_ref,
     s1_sem,
     s3_sem,
     gy_sem,
@@ -60,6 +65,8 @@
     far_sem,
     near_sem,
     rz_sem,
+    zf_sem,
+    yf_sem,
 ):
     rows, cols, n_noise, n_dp, kdim = cfg
     ys, zs = ring_sizes(n_dp)
@@ -227,6 +234,8 @@
         if i == 0:
             pl.semaphore_wait(barrier, n_noise - 1 + ys - 1 + zs - 1)
         waits.append(gather(ref, s1_sem.at[i], n_noise, me_n, peer_noise))
+    hrow, rhh = rows // 2, rch // 2
+    wait_y, gathered = [], ((gya_ref, gza_ref), (gyb_ref, gzb_ref))
     for i, (ref, out_ref) in enumerate(((st1a_ref, lsea_ref), (st1b_ref, lseb_ref))):
         waits[i]()
         g1.append(log_rows - joined(ref, n_noise))
@@ -237,7 +246,20 @@
         def write(chunk, line):
             out_ref[pl.ds(chunk, 1), :] = line
 
-        lse_pass(r_ref, i * hcol, hcol, q_ref, 0, rows, write)
+        if i == 0:
+            lse_pass(r_ref, 0, hcol, q_ref, 0, rows, write)
+            continue
+        for j in range(2):
+            lse_pass(
+                r_ref, hcol, hcol, q_ref, j * hrow, hrow, lambda c, x: write(j * rhh + c, x)
+            )
+            part = slice(j * rhh, (j + 1) * rhh)
+            one_half, other = lsea_ref[part], lseb_ref[part]
+            top = jnp.maximum(one_half, other)
+            total = jnp.exp2(one_half - top) + jnp.exp2(other - top)
+            lse_ref[part] = top + LOG2E * jnp.log(total)
+            gathered[j][0][me_y] = lse_ref[part]
+            wait_y.append(gather(gathered[j][0], gy_sem.at[j], ys, me_y, peer_y))
     g1 = jnp.concatenate(g1, axis=0)
 
     bl, bw, un = 256, cols, min(4, rows // 256)
@@ -256,20 +278,24 @@
         return carry
 
     steps = rows // (bl * un)
-    top = jnp.maximum(lsea_ref[...], lseb_ref[...])
-    lse = top + LOG2E * jnp.log(jnp.exp2(lsea_ref[...] - top) + jnp.exp2(lseb_ref[...] - top))
-    gy_ref[me_y] = lse
-    wait = gather(gy_ref, gy_sem, ys, me_y, peer_y)
+    lse = lse_ref[...]
     ul = ul_ref[...] - lse
     for c in range(rch):
         put_bias(q_ref, c, ul[c : c + 1, :], True)
-    lax.fori_loop(0, steps // 2, weights, 0)
-    wait()
-    gz_ref[me_z] = joined(gy_ref, ys)
-    wait = gather(gz_ref, gz_sem, zs, me_z, peer_z)
-    lax.fori_loop(steps // 2, steps, weights, 0)
-    wait()
-    rho_ref[...] = jnp.exp2(lse - joined(gz_ref, zs) + log_cols)
+    wait_z = []
+    done = 0
+    for j, (y_ref, z_ref) in enumerate(gathered):
+        upto = steps * (j + 1) // 4
+        lax.fori_loop(done, upto, weights, 0)
+        done = upto
+        wait_y[j]()
+        z_ref[me_z] = joined(y_ref, ys)
+        wait_z.append(gather(z_ref, gz_sem.at[j], zs, me_z, peer_z))
+    lax.fori_loop(done, steps, weights, 0)
+    for j in range(2):
+        wait_z[j]()
+        part = slice(j * rhh, (j + 1) * rhh)
+        rho_ref[part] = jnp.exp2(lse[part] - joined(gathered[j][1], zs) + log_cols)
 
     rho = rho_ref[...]
     rho_hi = rho.astype(jnp.bfloat16).astype(jnp.float32)
@@ -314,7 +340,8 @@
         offsets += [k, zs - k]
     offsets.append(0)
     pending = []
-    cuts = (pl.ds(0, 72), pl.ds(72, 64))
+    cuts = (pl.ds(0, 64), pl.ds(64, 56))
+    main, last = pl.ds(0, 120), pl.ds(120, 16)
 
     def send(src, dst, sem, device):
         copy = pltpu.make_async_remote_copy(
@@ -338,9 +365,9 @@
             line = rho_ref[pl.ds(y * zs + zt, 1), :]
             column = jnp.broadcast_to(line, (8, LANES)).T[:, 0:1]
             part = both[y * LANES : (y + 1) * LANES] * column
-            num_ref[zt, y, 0:64, :] = part[0:64, 0:128]
-            num_ref[zt, y, 64:72, :] = part[:, 128:136].T
-            num_ref[zt, y, 72:136, :] = part[64:128, 0:128]
+            num_ref[zt, y, 0:56, :] = part[0:56, 0:128]
+            num_ref[zt, y, 56:64, :] = part[:, 128:136].T
+            num_ref[zt, y, 64:136, :] = part[56:128, 0:128]
 
     def along(way, step):
         return (me_y + (step if way == 0 else ys - step)) % ys
@@ -388,30 +415,53 @@
             if ys == 4:
                 arrived(near_ref.at[way, i, cuts[way]], near_sem.at[way, i, 1])
         if ys == 4:
-            num_ref[zt, me_y] = num_ref[zt, me_y] + near_ref[0, i] + near_ref[1, i]
+            num_ref[zt, me_y, main] = num_ref[zt, me_y, main] + near_ref[0, i] + near_ref[1, i]
         else:
             for way in range(2):
                 part = cuts[1 - way]
                 num_ref[zt, me_y, part] = num_ref[zt, me_y, part] + near_ref[way, i, part]
         if offsets[i]:
-            send(num_ref.at[zt, me_y], rz_ref.at[i], rz_sem.at[i], peer_z(offsets[i]))
+            source = num_ref.at[zt, me_y, main]
+            send(source, rz_ref.at[i], rz_sem.at[i], peer_z(offsets[i]))
+
+    def z_first(i):
+        if offsets[i]:
+            source = num_ref.at[(me_z + offsets[i]) % zs, :, last]
+            send(source, zf_ref.at[i], zf_sem.at[i], peer_z(offsets[i]))
+
+    def z_merge():
+        total = num_ref[me_z, :, last]
+        for i in range(zs - 1):
+            arrived(zf_ref.at[i], zf_sem.at[i])
+            total = total + zf_ref[i]
+        num_ref[me_z, :, last] = total
+        for step in range(1, ys):
+            source = num_ref.at[me_z, (me_y + step) % ys, last]
+            send(source, yf_ref.at[step - 1], yf_sem.at[step - 1], peer_y(step))
 
     for i in range(zs):
         weigh(offsets[i])
         y_far(i)
+        z_first(i)
     for i in range(zs):
         y_near(i)
         y_forward(i)
+    z_merge()
     for i in range(zs):
         y_merge(i)
-    mine = num_ref[me_z, me_y]
+    rest = num_ref[me_z, me_y, last]
+    for step in range(1, ys):
+        arrived(yf_ref.at[step - 1], yf_sem.at[step - 1])
+        rest = rest + yf_ref[step - 1]
+    mine = num_ref[me_z, me_y, main]
     for i in range(zs - 1):
         arrived(rz_ref.at[i], rz_sem.at[i])
         mine = mine + rz_ref[i]
-    den = (mine[64:72]).T
+    den = (mine[56:64]).T
     den = den[:, 0:1] + den[:, 1:2]
-    targets_ref[0:64, :] = mine[0:64] / den[0:64]
-    targets_ref[64:128, :] = mine[72:136] / den[64:128]
+    targets_ref[0:56, :] = mine[0:56] / den[0:56]
+    targets_ref[56:112, :] = mine[64:120] / den[56:112]
+    targets_ref[112:128, :] = rest / den[112:128]
     for copy in pending:
         copy.wait_send()
 
@@ -430,8 +480,8 @@
     targets, pot = pl.pallas_call(
         functools.partial(kernel, cfg),
         out_shape=(
-            jax.ShapeDtypeStruct((LANES, width), f32),
-            jax.ShapeDtypeStruct((cch, LANES), f32),
+            pltpu.VMEM((LANES, width), f32),
+            pltpu.VMEM((cch, LANES), f32),
         ),
         in_specs=[vmem] * 3,
         out_specs=(vmem, vmem),
@@ -448,20 +498,27 @@
             pltpu.VMEM((rch, LANES), f32),
             pltpu.VMEM((rch, LANES), f32),
             pltpu.VMEM((rch, LANES), f32),
-            pltpu.VMEM((ys, rch, LANES), f32),
-            pltpu.VMEM((zs, rch, LANES), f32),
+            pltpu.VMEM((rch, LANES), f32),
+            pltpu.VMEM((ys, rch // 2, LANES), f32),
+            pltpu.VMEM((ys, rch // 2, LANES), f32),
+            pltpu.VMEM((zs, rch // 2, LANES), f32),
+            pltpu.VMEM((zs, rch // 2, LANES), f32),
             pltpu.VMEM((n_noise, cch, LANES), f32),
             pltpu.VMEM((zs, ys, 136, LANES), f32),
-            pltpu.VMEM((zs, 136, LANES), f32),
-            pltpu.VMEM((2, zs, 136, LANES), f32),
-            pltpu.VMEM((zs - 1, 136, LANES), f32),
+            pltpu.VMEM((zs, 120, LANES), f32),
+            pltpu.VMEM((2, zs, 120, LANES), f32),
+            pltpu.VMEM((zs - 1, 120, LANES), f32),
+            pltpu.VMEM((zs - 1, ys, 16, LANES), f32),
+            pltpu.VMEM((ys - 1, 16, LANES), f32),
             dma((2, 2, n_noise)),
             dma((2, n_noise)),
-            dma((2, ys)),
-            dma((2, zs)),
+            dma((2, 2, ys)),
+            dma((2, 2, zs)),
             dma((zs, 2, 2)),
             dma((2, zs, 2, 2)),
             dma((zs - 1, 2)),
+            dma((zs - 1, 2)),
+            dma((ys - 1, 2)),
         ],
         compiler_params=pltpu.CompilerParams(
             collective_id=0, has_side_effects=True, vmem_limit_bytes=56 * 2**20

time: 77.9 us -> 73.4 us (0.942)
  Pallas kernels: 75 us -> 71.4 us
  local copies, waits for them, and re-layouts: 2.08 us -> 1.23 us
    pallas_call x1, Pallas kernels: 75 us -> 71.4 us  [shards(): pl.pallas_call(functools.partial(kernel, cfg), out_shape=(pltpu.VMEM((LAN...]
    unnamed x4 -> x2, local copies, waits for them, and re-layouts: 2.08 us -> 1.23 us
where the time goes in v5:
time: 73.4 us; the launch traced here: 73.3 us
  Pallas kernels  71.4 us (97%)
  local copies, waits for them, and re-layouts  1.23 us (2%)
    pallas_call x1, Pallas kernels, shards(): pl.pallas_call(functools.partial(kernel, cfg), out_shape=(pltpu.VMEM((LAN...  71.4 us

profile of v5, /device:TPU:1, one launch (start us, length us, event | category | flops | bytes accessed | tf_op | source)
XLA Modules:
  0.0 73.3 jit_solution(9447416777280233445)
XLA Ops:
  0.6 71.4 %shard_map.50 = (f32[128,128]{1,0:T(8,128)S(1)}, f32[16,128]{1,0:T(8,128)S(1)}) custom-call(bf16[4096,128]{1,0:T(8,128)(2,1)} %noise_ref.1, bf16[2048,128]{1,0:T(8,128)(2,1)} %data_ref.1, bf16[64,128]{1,0:T(8,128)(2,1)} %bitcast.3), custom_call_target="tpu_custom_call" | custom-call | flops 17179869184 | bytes 2097152 | tf_op jit(solution)/shard_map/pallas_call | solution.py:480
  72.0 0.6 copy.7
  72.7 0.6 copy.8

commit v6 on v5

--- a/solution.py
+++ b/solution.py
@@ -292,24 +292,27 @@
         z_ref[me_z] = joined(y_ref, ys)
         wait_z.append(gather(z_ref, gz_sem.at[j], zs, me_z, peer_z))
     lax.fori_loop(done, steps, weights, 0)
+    hys = ys // 2
+    zero6 = jnp.zeros((6, hys * LANES), jnp.float32)
+    total = jnp.zeros((8, cols), jnp.float32)
     for j in range(2):
         wait_z[j]()
         part = slice(j * rhh, (j + 1) * rhh)
-        rho_ref[part] = jnp.exp2(lse[part] - joined(gathered[j][1], zs) + log_cols)
-
-    rho = rho_ref[...]
-    rho_hi = rho.astype(jnp.bfloat16).astype(jnp.float32)
-    rho_lo = rho - rho_hi
-    zero6 = jnp.zeros((6, ys * LANES), jnp.float32)
-    total = jnp.zeros((8, cols), jnp.float32)
-    for z in range(zs):
-        lines = []
-        for part in (rho_hi, rho_lo):
-            lines.append(
-                jnp.concatenate([part[y * zs + z : y * zs + z + 1] for y in range(ys)], axis=1)
-            )
-        lhs = jnp.concatenate(lines + [zero6], axis=0).astype(jnp.bfloat16)
-        total = total + jnp.dot(lhs, p_ref[z], preferred_element_type=jnp.float32)
+        rho = jnp.exp2(lse[part] - joined(gathered[j][1], zs) + log_cols)
+        rho_ref[part] = rho
+        rho_hi = rho.astype(jnp.bfloat16).astype(jnp.float32)
+        rho_lo = rho - rho_hi
+        for z in range(zs):
+            lines = []
+            for half_rho in (rho_hi, rho_lo):
+                lines.append(
+                    jnp.concatenate(
+                        [half_rho[y * zs + z : y * zs + z + 1] for y in range(hys)], axis=1
+                    )
+                )
+            lhs = jnp.concatenate(lines + [zero6], axis=0).astype(jnp.bfloat16)
+            block = p_ref[z, j * hys * LANES : (j + 1) * hys * LANES]
+            total = total + jnp.dot(lhs, block, preferred_element_type=jnp.float32)
     total = total[0:1] + total[1:2]
     for c in range(cch):
         st3_ref[me_n, c : c + 1, :] = total[:, c * LANES : (c + 1) * LANES]
@@ -317,7 +320,6 @@
     total = st3_ref[0]
     for k in range(1, n_noise):
         total = total + st3_ref[k]
-    pot_ref[...] = (epsilon * LN2) * (g1 + log_rows - jnp.log(total) * LOG2E)
 
     factor = float(rows * n_noise) / total
     f_hi = factor.astype(jnp.bfloat16).astype(jnp.float32)
@@ -340,8 +342,8 @@
         offsets += [k, zs - k]
     offsets.append(0)
     pending = []
-    cuts = (pl.ds(0, 64), pl.ds(64, 56))
-    main, last = pl.ds(0, 120), pl.ds(120, 16)
+    cuts = (pl.ds(0, 56), pl.ds(56, 56))
+    main, last = pl.ds(0, 112), pl.ds(112, 24)
 
     def send(src, dst, sem, device):
         copy = pltpu.make_async_remote_copy(
@@ -365,9 +367,9 @@
             line = rho_ref[pl.ds(y * zs + zt, 1), :]
             column = jnp.broadcast_to(line, (8, LANES)).T[:, 0:1]
             part = both[y * LANES : (y + 1) * LANES] * column
-            num_ref[zt, y, 0:56, :] = part[0:56, 0:128]
-            num_ref[zt, y, 56:64, :] = part[:, 128:136].T
-            num_ref[zt, y, 64:136, :] = part[56:128, 0:128]
+            num_ref[zt, y, 0:48, :] = part[0:48, 0:128]
+            num_ref[zt, y, 48:56, :] = part[:, 128:136].T
+            num_ref[zt, y, 56:136, :] = part[48:128, 0:128]
 
     def along(way, step):
         return (me_y + (step if way == 0 else ys - step)) % ys
@@ -446,9 +448,13 @@
     for i in range(zs):
         y_near(i)
         y_forward(i)
-    z_merge()
+    pot_ref[...] = (epsilon * LN2) * (g1 + log_rows - jnp.log(total) * LOG2E)
     for i in range(zs):
+        if i == zs // 2:
+            z_merge()
         y_merge(i)
+    for copy in pending:
+        copy.wait_send()
     rest = num_ref[me_z, me_y, last]
     for step in range(1, ys):
         arrived(yf_ref.at[step - 1], yf_sem.at[step - 1])
@@ -457,13 +463,11 @@
     for i in range(zs - 1):
         arrived(rz_ref.at[i], rz_sem.at[i])
         mine = mine + rz_ref[i]
-    den = (mine[56:64]).T
+    den = (mine[48:56]).T
     den = den[:, 0:1] + den[:, 1:2]
-    targets_ref[0:56, :] = mine[0:56] / den[0:56]
-    targets_ref[56:112, :] = mine[64:120] / den[56:112]
-    targets_ref[112:128, :] = rest / den[112:128]
-    for copy in pending:
-        copy.wait_send()
+    targets_ref[0:48, :] = mine[0:48] / den[0:48]
+    targets_ref[48:104, :] = mine[56:112] / den[48:104]
+    targets_ref[104:128, :] = rest / den[104:128]
 
 
 def shards(noise_latents, data_latents, projection):
@@ -505,11 +509,11 @@
             pltpu.VMEM((zs, rch // 2, LANES), f32),
             pltpu.VMEM((n_noise, cch, LANES), f32),
             pltpu.VMEM((zs, ys, 136, LANES), f32),
-            pltpu.VMEM((zs, 120, LANES), f32),
-            pltpu.VMEM((2, zs, 120, LANES), f32),
-            pltpu.VMEM((zs - 1, 120, LANES), f32),
-            pltpu.VMEM((zs - 1, ys, 16, LANES), f32),
-            pltpu.VMEM((ys - 1, 16, LANES), f32),
+            pltpu.VMEM((zs, 112, LANES), f32),
+            pltpu.VMEM((2, zs, 112, LANES), f32),
+            pltpu.VMEM((zs - 1, 112, LANES), f32),
+            pltpu.VMEM((zs - 1, ys, 24, LANES), f32),
+            pltpu.VMEM((ys - 1, 24, LANES), f32),
             dma((2, 2, n_noise)),
             dma((2, n_noise)),
             dma((2, 2, ys)),

time: 73.4 us -> 71.7 us (0.977)
  Pallas kernels: 71.4 us -> 69.7 us
    pallas_call x1, Pallas kernels: 71.4 us -> 69.7 us  [shards(): pl.pallas_call(functools.partial(kernel, cfg), out_shape=(pltpu.VMEM((LAN...]
where the time goes in v6:
time: 71.7 us; the launch traced here: 71.6 us
  Pallas kernels  69.7 us (97%)
  local copies, waits for them, and re-layouts  1.23 us (2%)
    pallas_call x1, Pallas kernels, shards(): pl.pallas_call(functools.partial(kernel, cfg), out_shape=(pltpu.VMEM((LAN...  69.7 us

profile of v6, /device:TPU:1, one launch (start us, length us, event | category | flops | bytes accessed | tf_op | source)
XLA Modules:
  0.0 71.6 jit_solution(5221929818721762410)
XLA Ops:
  0.6 69.7 %shard_map.50 = (f32[128,128]{1,0:T(8,128)S(1)}, f32[16,128]{1,0:T(8,128)S(1)}) custom-call(bf16[4096,128]{1,0:T(8,128)(2,1)} %noise_ref.1, bf16[2048,128]{1,0:T(8,128)(2,1)} %data_ref.1, bf16[64,128]{1,0:T(8,128)(2,1)} %bitcast.3), custom_call_target="tpu_custom_call" | custom-call | flops 17179869184 | bytes 2097152 | tf_op jit(solution)/shard_map/pallas_call | solution.py:484
  70.4 0.6 copy.7
  71.0 0.6 copy.8

commit v7 on v6

--- a/solution.py
+++ b/solution.py
@@ -29,11 +29,14 @@
 
 def kernel(
     cfg,
+    noise_in,
+    data_in,
+    proj_in,
+    targets_ref,
+    pot_ref,
     noise_ref,
     data_ref,
     proj_ref,
-    targets_ref,
-    pot_ref,
     q_ref,
     r_ref,
     p_ref,
@@ -58,6 +61,9 @@
     rz_ref,
     zf_ref,
     yf_ref,
+    den_ref,
+    dy_ref,
+    dz_ref,
     s1_sem,
     s3_sem,
     gy_sem,
@@ -67,6 +73,9 @@
     rz_sem,
     zf_sem,
     yf_sem,
+    dy_sem,
+    dz_sem,
+    in_sem,
 ):
     rows, cols, n_noise, n_dp, kdim = cfg
     ys, zs = ring_sizes(n_dp)
@@ -88,6 +97,20 @@
     def peer_z(step):
         return (me_n, me_y * zs + (me_z + step) % zs)
 
+    hrow = rows // 2
+    loads = [
+        pltpu.make_async_copy(src, dst, in_sem.at[i])
+        for i, (src, dst) in enumerate(
+            (
+                (proj_in, proj_ref),
+                (data_in, data_ref),
+                (noise_in.at[0:hrow], noise_ref.at[0:hrow]),
+                (noise_in.at[hrow:rows], noise_ref.at[hrow:rows]),
+            )
+        )
+    ]
+    for load in loads:
+        load.start()
     barrier = pltpu.get_barrier_semaphore()
 
     def greet_noise(k, carry):
@@ -106,6 +129,7 @@
     lax.fori_loop(1, ys, greet_y, 0)
     lax.fori_loop(1, zs, greet_z, 0)
 
+    loads[0].wait()
     proj2_ref[0:kdim, :] = proj_ref[...]
     proj2_ref[kdim : 2 * kdim, :] = proj_ref[...]
     half = jnp.full((8, LANES), 0.5, jnp.bfloat16)
@@ -118,11 +142,11 @@
         tile = jnp.concatenate((parts + ones if first else ones + parts) + [zero], axis=0)
         dst_ref[c * LANES : (c + 1) * LANES, 128:136] = tile.T.astype(jnp.bfloat16)
 
-    def prepare(src_ref, dst_ref, bias_ref, count, is_q):
-        step = min(2048, count)
-
-        def body(b, carry):
-            sl = pl.ds(pl.multiple_of(b * step, step), step)
+    def prepare(src_ref, dst_ref, bias_ref, count, is_q, parts):
+        step = count // len(parts)
+        for b, load in enumerate(parts):
+            load.wait()
+            sl = pl.ds(b * step, step)
             proj = lax.dot_general(
                 src_ref[sl, :], proj2_ref[...], NT, preferred_element_type=jnp.float32
             )
@@ -149,15 +173,12 @@
                 bias_ref[pl.ds(b * (step // LANES) + c, 1), :] = (
                     -norm_scale * norm[0:1, c * LANES : (c + 1) * LANES]
                 )
-            return carry
-
-        lax.fori_loop(0, count // step, body, 0)
         bias = bias_ref[...]
         for c in range(count // LANES):
             put_bias(dst_ref, c, bias[c : c + 1, :], is_q)
 
-    prepare(noise_ref, q_ref, ul_ref, rows, True)
-    prepare(data_ref, r_ref, vl_ref, cols, False)
+    prepare(data_ref, r_ref, vl_ref, cols, False, loads[1:2])
+    prepare(noise_ref, q_ref, ul_ref, rows, True, loads[2:4])
 
     def lse_pass(lhs_ref, first, count, rhs_ref, start, width, write):
         bw = min(2048, width)
@@ -234,7 +255,7 @@
         if i == 0:
             pl.semaphore_wait(barrier, n_noise - 1 + ys - 1 + zs - 1)
         waits.append(gather(ref, s1_sem.at[i], n_noise, me_n, peer_noise))
-    hrow, rhh = rows // 2, rch // 2
+    rhh = rch // 2
     wait_y, gathered = [], ((gya_ref, gza_ref), (gyb_ref, gzb_ref))
     for i, (ref, out_ref) in enumerate(((st1a_ref, lsea_ref), (st1b_ref, lseb_ref))):
         waits[i]()
@@ -342,8 +363,8 @@
         offsets += [k, zs - k]
     offsets.append(0)
     pending = []
-    cuts = (pl.ds(0, 56), pl.ds(56, 56))
-    main, last = pl.ds(0, 112), pl.ds(112, 24)
+    cuts = (pl.ds(0, 56), pl.ds(56, 48))
+    main, last = pl.ds(0, 104), pl.ds(104, 24)
 
     def send(src, dst, sem, device):
         copy = pltpu.make_async_remote_copy(
@@ -367,9 +388,9 @@
             line = rho_ref[pl.ds(y * zs + zt, 1), :]
             column = jnp.broadcast_to(line, (8, LANES)).T[:, 0:1]
             part = both[y * LANES : (y + 1) * LANES] * column
-            num_ref[zt, y, 0:48, :] = part[0:48, 0:128]
-            num_ref[zt, y, 48:56, :] = part[:, 128:136].T
-            num_ref[zt, y, 56:136, :] = part[48:128, 0:128]
+            num_ref[zt, y] = part[:, 0:128]
+            sums = part[:, 128:136].T
+            den_ref[y, zt] = sums[0:1] + sums[1:2]
 
     def along(way, step):
         return (me_y + (step if way == 0 else ys - step)) % ys
@@ -431,6 +452,21 @@
             source = num_ref.at[(me_z + offsets[i]) % zs, :, last]
             send(source, zf_ref.at[i], zf_sem.at[i], peer_z(offsets[i]))
 
+    def den_first():
+        for step in range(1, ys):
+            source = den_ref.at[(me_y + step) % ys]
+            send(source, dy_ref.at[step - 1], dy_sem.at[step - 1], peer_y(step))
+
+    def den_merge():
+        total = den_ref[me_y]
+        for step in range(1, ys):
+            arrived(dy_ref.at[step - 1], dy_sem.at[step - 1])
+            total = total + dy_ref[step - 1]
+        den_ref[me_y] = total
+        for i in range(zs - 1):
+            source = den_ref.at[me_y, (me_z + offsets[i]) % zs]
+            send(source, dz_ref.at[i], dz_sem.at[i], peer_z(offsets[i]))
+
     def z_merge():
         total = num_ref[me_z, :, last]
         for i in range(zs - 1):
@@ -445,9 +481,11 @@
         weigh(offsets[i])
         y_far(i)
         z_first(i)
+    den_first()
     for i in range(zs):
         y_near(i)
         y_forward(i)
+    den_merge()
     pot_ref[...] = (epsilon * LN2) * (g1 + log_rows - jnp.log(total) * LOG2E)
     for i in range(zs):
         if i == zs // 2:
@@ -459,14 +497,16 @@
     for step in range(1, ys):
         arrived(yf_ref.at[step - 1], yf_sem.at[step - 1])
         rest = rest + yf_ref[step - 1]
+    den = den_ref[me_y, me_z]
+    for i in range(zs - 1):
+        arrived(dz_ref.at[i], dz_sem.at[i])
+        den = den + dz_ref[i]
+    den = jnp.broadcast_to(den, (8, LANES)).T[:, 0:1]
     mine = num_ref[me_z, me_y, main]
     for i in range(zs - 1):
         arrived(rz_ref.at[i], rz_sem.at[i])
         mine = mine + rz_ref[i]
-    den = (mine[48:56]).T
-    den = den[:, 0:1] + den[:, 1:2]
-    targets_ref[0:48, :] = mine[0:48] / den[0:48]
-    targets_ref[48:104, :] = mine[56:112] / den[48:104]
+    targets_ref[0:104, :] = mine / den[0:104]
     targets_ref[104:128, :] = rest / den[104:128]
 
 
@@ -487,9 +527,12 @@
             pltpu.VMEM((LANES, width), f32),
             pltpu.VMEM((cch, LANES), f32),
         ),
-        in_specs=[vmem] * 3,
+        in_specs=[pl.BlockSpec(memory_space=pl.ANY)] * 3,
         out_specs=(vmem, vmem),
         scratch_shapes=[
+            pltpu.VMEM((rows, width), bf16),
+            pltpu.VMEM((cols, width), bf16),
+            pltpu.VMEM((kdim, width), bf16),
             pltpu.VMEM((rows, 256), bf16),
             pltpu.VMEM((cols, 256), bf16),
             pltpu.VMEM((zs, ys * LANES, cols), bf16),
@@ -508,12 +551,15 @@
             pltpu.VMEM((zs, rch // 2, LANES), f32),
             pltpu.VMEM((zs, rch // 2, LANES), f32),
             pltpu.VMEM((n_noise, cch, LANES), f32),
-            pltpu.VMEM((zs, ys, 136, LANES), f32),
-            pltpu.VMEM((zs, 112, LANES), f32),
-            pltpu.VMEM((2, zs, 112, LANES), f32),
-            pltpu.VMEM((zs - 1, 112, LANES), f32),
+            pltpu.VMEM((zs, ys, LANES, LANES), f32),
+            pltpu.VMEM((zs, 104, LANES), f32),
+            pltpu.VMEM((2, zs, 104, LANES), f32),
+            pltpu.VMEM((zs - 1, 104, LANES), f32),
             pltpu.VMEM((zs - 1, ys, 24, LANES), f32),
             pltpu.VMEM((ys - 1, 24, LANES), f32),
+            pltpu.VMEM((ys, zs, 1, LANES), f32),
+            pltpu.VMEM((ys - 1, zs, 1, LANES), f32),
+            pltpu.VMEM((zs - 1, 1, LANES), f32),
             dma((2, 2, n_noise)),
             dma((2, n_noise)),
             dma((2, 2, ys)),
@@ -523,6 +569,9 @@
             dma((zs - 1, 2)),
             dma((zs - 1, 2)),
             dma((ys - 1, 2)),
+            dma((ys - 1, 2)),
+            dma((zs - 1, 2)),
+            dma((4,)),
         ],
         compiler_params=pltpu.CompilerParams(
             collective_id=0, has_side_effects=True, vmem_limit_bytes=56 * 2**20

time: 71.7 us -> 71.2 us (level)
  no operation moved by 1% of the time
where the time goes in v7:
time: 71.2 us; the launch traced here: 71 us
  Pallas kernels  69.2 us (97%)
  local copies, waits for them, and re-layouts  1.23 us (2%)
    pallas_call x1, Pallas kernels, shards(): pl.pallas_call(functools.partial(kernel, cfg), out_shape=(pltpu.VMEM((LAN...  69.2 us

profile of v7, /device:TPU:1, one launch (start us, length us, event | category | flops | bytes accessed | tf_op | source)
XLA Modules:
  0.0 71.0 jit_solution(13433738615096140577)
XLA Ops:
  0.6 69.2 %shard_map.50 = (f32[128,128]{1,0:T(8,128)S(1)}, f32[16,128]{1,0:T(8,128)S(1)}) custom-call(bf16[4096,128]{1,0:T(8,128)(2,1)} %noise_in.1, bf16[2048,128]{1,0:T(8,128)(2,1)} %data_in.1, bf16[64,128]{1,0:T(8,128)(2,1)} %bitcast.3), custom_call_target="tpu_custom_call" | custom-call | flops 17179869184 | bytes 2097152 | tf_op jit(solution)/shard_map/pallas_call | solution.py:524
  69.8 0.6 copy.7
  70.4 0.6 copy.8
